TPU v7x, 256 devices: a whole 4x4x8 slice. The times are simulated.
256 devices in a mesh: sec: 8 (over y, z_hi), row: 4 (over x), col: 8 (over z_lo, core).
Axes of the slice: x: 4, y: 4, z: 8 (z_hi: 2, z_lo: 4; z = z_hi * 4 + z_lo), core: 2. Of those that a mesh axis runs over, the one named last changes fastest.
Arguments:
- pairs: float32 [8, 2, 2048, 4096], P('sec', None, 'row', 'col'), may hold values from -0.75 to 0.75
Outputs:
- combined: float32 [8, 2, 2048, 4096], P('sec', None, 'row', 'col')
All inputs are finite; a program needn't handle non-finite values.
Results may differ from a plain program's by a relative error of at most 0.0001.
Values sent between devices are 32-bit elements; how exact they have to be, the bound alone decides.
No kernel may reach another device: no remote copies, remote signals or barrier semaphores. Data moves between devices by JAX's collectives and lax.ppermute only.
A program may use at most 128 MiB of HBM per device.

v0:
```python
import jax
import jax.numpy as jnp
from jax import lax
from jax.sharding import PartitionSpec as P


def from_partner(x, axis, stride):
    return lax.ppermute(x, axis, [(i, i ^ 1 << stride) for i in range(lax.axis_size(axis))])


def real_dot(left, right):
    return jnp.dot(left, right, precision=lax.Precision.HIGHEST, preferred_element_type=jnp.float32)


def real_form(columns):
    block_width = columns.shape[2] // 2
    blocks = columns.shape[1] // block_width
    shaped = columns.reshape(2, blocks, block_width, 2 * block_width)
    real_part = shaped[:, :, :, :block_width]
    imag_part = shaped[:, :, :, block_width:]
    lower = jnp.concatenate([-imag_part, real_part], axis=3)
    stacked = jnp.stack([shaped, lower], axis=2)
    return stacked.reshape(2, 2 * columns.shape[1], 2 * block_width)


def accumulate(block_piece, expanded):
    product = real_dot(block_piece[0], expanded[0])
    derivative = real_dot(block_piece[1], expanded[0]) + real_dot(block_piece[0], expanded[1])
    return (product, derivative)


def shards(pairs):
    own_pair = pairs[0]
    partner = from_partner(own_pair, "sec", 0)
    parity = lax.axis_index("sec") % 2
    first_pair = jnp.where(parity == 0, own_pair, partner)
    second_pair = jnp.where(parity == 0, partner, own_pair)
    columns = lax.all_gather(second_pair, "row", axis=1, tiled=True)
    expanded = real_form(columns)
    totals = accumulate(lax.all_gather(first_pair, "col", axis=2, tiled=True), expanded)
    combined = jnp.stack([totals[0], totals[1]])
    return combined[None]


def solution(mesh):
    placed = (P("sec", None, "row", "col"),)
    return jax.shard_map(
        shards, mesh=mesh, in_specs=placed, out_specs=P("sec", None, "row", "col"), check_vma=False
    )
```

profile of v0, /device:TPU:1, one launch (start us, length us, event | category | flops | bytes accessed | tf_op | source)
XLA Modules:
  0.0 424.1 jit_solution(3735169528564480768)
XLA Ops:
  6.5 0.0 all-gather.5.cloned.1.call-start
  6.5 7.7 %collective-permute-start = (f32[2,512,512]{2,1,0:T(8,128)}, f32[2,512,512]{2,1,0:T(8,128)S(1)}, u32[]{:S(2)}, u32[]{:S(2)}) collective-permute-start(f32[2,512,512]{2,1,0:T(8,128)} %bitcast.40), channel_id=1, source_target_pairs={{0,32},{32,0},{64,96},{96,64},{128,160},{160,128},{192,224},{224,1... | collective-permute-start | bytes 6291464 | tf_op jit(solution)/shard_map/ppermute | solution.py:8
  14.3 61.2 %collective-permute-done = f32[2,512,512]{2,1,0:T(8,128)S(1)} collective-permute-done((f32[2,512,512]{2,1,0:T(8,128)}, f32[2,512,512]{2,1,0:T(8,128)S(1)}, u32[]{:S(2)}, u32[]{:S(2)}) %collective-permute-start) | collective-permute-done | bytes 2097184 | tf_op jit(solution)/shard_map/ppermute | solution.py:8
  75.5 4.4 %broadcast_select_fusion.1 = (f32[2,512,512]{2,1,0:T(8,128)}, f32[2,512,512]{2,1,0:T(8,128)}) fusion(f32[2,512,512]{2,1,0:T(8,128)S(1)} %collective-permute-done, pred[]{:T(512)S(6)} %eq.6, f32[1,2,512,512]{3,2,1,0:T(8,128)} %param.1), kind=kLoop, calls=%fused_computation.16 | loop fusion | flops 1048576 | bytes 8388609 | tf_op jit(solution)/shard_map/jit(_where)/select_n | solution.py:36
  79.9 0.0 all-gather.5.cloned.1.call-update
  79.9 0.0 all-gather.3.cloned.1.call-start
  80.0 0.7 all-gather.3.cloned.1.call-update
  80.7 116.1 %all-gather.5.cloned.1.call-done = f32[2,2048,512]{2,1,0:T(8,128)} async-done(((f32[2,512,512]{2,1,0:T(8,128)}), f32[2,2048,512]{2,1,0:T(8,128)}) %all-gather.5.cloned.1.call-update) | async-done | bytes 8388624 | tf_op jit(solution)/shard_map/all_gather | solution.py:38
  196.8 0.0 slice-start.2
  196.8 6.5 %slice_negate_fusion = (f32[2,8,256,256]{3,2,1,0:T(8,128)S(1)}, f32[2,8,256,256]{3,2,1,0:T(8,128)}) fusion(f32[2,8,256,512]{3,2,1,0:T(8,128)} %bitcast.36), kind=kLoop, calls=%fused_computation.10 | loop fusion | flops 1048576 | bytes 16777216 | tf_op jit(solution)/shard_map/neg | solution.py:21
  203.3 0.0 slice-start.3
  203.3 6.9 %maximum_bitcast_fusion = f32[2,8,1,256,512]{4,3,2,1,0:T(8,128)} fusion(f32[2,8,256,256]{3,2,1,0:T(8,128)} %get-tuple-element.8, f32[2,8,256,256]{3,2,1,0:T(8,128)S(1)} %get-tuple-element.7), kind=kLoop, calls=%fused_computation.7 | loop fusion | flops 2097152 | bytes 16777216 | tf_op jit(solution)/shard_map/stack | solution.py:22
  210.2 0.0 slice-done.2
  210.2 0.0 slice-done.3
  210.2 10.3 %fusion = (f32[1,8,2,256,512]{4,3,2,1,0:T(8,128)}, f32[1,8,2,256,512]{4,3,2,1,0:T(8,128)}) fusion(f32[2,8,1,256,512]{4,3,2,1,0:T(8,128)S(1)} %bitcast.39, f32[2,8,1,256,512]{4,3,2,1,0:T(8,128)} %maximum_bitcast_fusion), kind=kLoop, calls=%fused_computation.2 | loop fusion | flops 4194304 | bytes 33554432 | tf_op jit(solution)/shard_map/stack | solution.py:22
  220.4 149.5 %all-gather.3.cloned.1.call-done = f32[2,512,4096]{2,1,0:T(8,128)} async-done(((f32[2,512,512]{2,1,0:T(8,128)}), f32[2,512,4096]{2,1,0:T(8,128)}) %all-gather.3.cloned.1.call-update) | async-done | bytes 16777232 | tf_op jit(solution)/shard_map/all_gather | solution.py:40
  369.9 0.0 copy-start
  369.9 0.0 copy-start.1
  369.9 0.0 slice-start
  369.9 16.5 %fusion.4 = f32[1,512,512]{2,1,0:T(8,128)S(1)} fusion(f32[4096,512]{1,0:T(8,128)} %bitcast.31, f32[2,512,4096]{2,1,0:T(8,128)} %all-gather.3.cloned.1.call-done), kind=kOutput, calls=%fused_computation.12 | convolution fusion | flops 12884901888 | bytes 17825792 | tf_op jit(solution)/shard_map/dot_general | solution.py:12
  386.5 0.0 slice-start.1
  386.5 0.0 copy-done
  386.5 0.0 copy-done.1
  386.5 14.2 %fusion.2 = f32[512,512]{1,0:T(8,128)S(1)} fusion(f32[4096,512]{1,0:T(8,128)S(1)} %bitcast.35, f32[2,512,4096]{2,1,0:T(8,128)S(1)} %copy-done), kind=kOutput, calls=%fused_computation.8 | convolution fusion | flops 12884901888 | bytes 17825792 | tf_op jit(solution)/shard_map/dot_general | solution.py:12
  400.7 0.0 slice-done
  400.7 0.0 slice-done.1
  400.7 15.1 %fusion.6 = f32[1,512,512]{2,1,0:T(8,128)S(1)} fusion(f32[512,512]{1,0:T(8,128)S(1)} %fusion.2, f32[4096,512]{1,0:T(8,128)S(1)} %bitcast.34, f32[2,512,4096]{2,1,0:T(8,128)S(1)} %copy-done), kind=kOutput, calls=%fused_computation.14 | convolution fusion | flops 12885164032 | bytes 18874368 | tf_op jit(solution)/shard_map/dot_general | solution.py:12
  415.8 1.5 maximum_bitcast_fusion.1
  (2 shorter events, 0.0 us)
Async XLA Ops:
  6.5 190.3 %all-gather.5.cloned.1.call-start = ((), (), s32[]{:S(2)}) async-start(), calls=%async_computation.1 | async-start | bytes 10485760 | tf_op jit(solution)/shard_map/all_gather | solution.py:38
  6.5 69.0 %collective-permute-start = (f32[2,512,512]{2,1,0:T(8,128)}, f32[2,512,512]{2,1,0:T(8,128)S(1)}, u32[]{:S(2)}, u32[]{:S(2)}) collective-permute-start(f32[2,512,512]{2,1,0:T(8,128)} %bitcast.40), channel_id=1, source_target_pairs={{0,32},{32,0},{64,96},{96,64},{128,160},{160,128},{192,224},{224,1... | collective-permute-start | bytes 6291464 | tf_op jit(solution)/shard_map/ppermute | solution.py:8
  79.9 290.0 %all-gather.3.cloned.1.call-start = ((), (), s32[]{:S(2)}) async-start(), calls=%async_computation | async-start | bytes 18874368 | tf_op jit(solution)/shard_map/all_gather | solution.py:40
  196.8 13.4 %slice-start.2 = ((s8[8388608]{0:T(1024)(128)(4,1)}), s8[4194304]{0:T(1024)(128)(4,1)S(1)}, s32[]{:S(2)}) async-start(s8[8388608]{0:T(1024)(128)(4,1)} %bitcast.37), calls=%async_computation.4 | async-start | bytes 8388608
  203.3 6.9 %slice-start.3 = ((s8[8388608]{0:T(1024)(128)(4,1)}), s8[4194304]{0:T(1024)(128)(4,1)S(1)}, s32[]{:S(2)}) async-start(s8[8388608]{0:T(1024)(128)(4,1)} %bitcast.37), calls=%async_computation.5 | async-start | bytes 8388608
  369.9 16.5 %copy-start = (f32[2,512,4096]{2,1,0:T(8,128)S(1)}, f32[2,512,4096]{2,1,0:T(8,128)}, u32[]{:S(2)}) copy-start(f32[2,512,4096]{2,1,0:T(8,128)} %all-gather.3.cloned.1.call-done) | copy-start | bytes 50331652
  369.9 16.6 %copy-start.1 = (f32[1,8,2,256,512]{4,3,2,1,0:T(8,128)S(1)}, f32[1,8,2,256,512]{4,3,2,1,0:T(8,128)}, u32[]{:S(2)}) copy-start(f32[1,8,2,256,512]{4,3,2,1,0:T(8,128)} %get-tuple-element.6) | copy-start | bytes 25165828
  369.9 30.7 %slice-start = ((s8[8388608]{0:T(1024)(128)(4,1)}), s8[4194304]{0:T(1024)(128)(4,1)S(1)}, s32[]{:S(2)}) async-start(s8[8388608]{0:T(1024)(128)(4,1)} %bitcast.32), calls=%async_computation.2 | async-start | bytes 8388608
  386.5 14.2 %slice-start.1 = ((s8[8388608]{0:T(1024)(128)(4,1)}), s8[4194304]{0:T(1024)(128)(4,1)S(1)}, s32[]{:S(2)}) async-start(s8[8388608]{0:T(1024)(128)(4,1)} %bitcast.32), calls=%async_computation.3 | async-start | bytes 8388608
Sparse Core Ops, SparseCore 0:
  80.0 116.7 all-gather.4
  198.6 171.2 all-gather.2
where the time goes:
time: 426 us; the launch traced here: 424 us
  waiting for transfers between devices  328 us (77%)
  matrix products  45.8 us (11%)
  other arithmetic  29.5 us (7%)
  between operations  13.5 us (3%)
  starting transfers between devices  7.78 us (2%)
    all_gather x1, waiting for transfers between devices, shards(): lax.all_gather(first_pair, 'col', axis=2, tiled=True)  149 us
    all_gather x1, waiting for transfers between devices, shards(): columns = lax.all_gather(second_pair, 'row', axis=1, tiled=True)  116 us
    ppermute x1, waiting for transfers between devices, from_partner(): lax.ppermute(x, axis, [(i, i ^ 1 << stride) for i in range(lax.axis_size(...  61.2 us
    dot_general x3, matrix products, real_dot(): jnp.dot(left, right, precision=lax.Precision.HIGHEST, preferred_element_t...  45.8 us
    another operation x2, other arithmetic, real_form(): stacked = jnp.stack([shaped, lower], axis=2)  17.1 us
  transfers between devices with their start and end apart: 3, of which 3 were waited for; matrix products, arithmetic and copies ran while one was open for 6% of the time, Pallas kernels for 0%

commit v1 on v0

v1 whole, which is shorter than its diff:
```python
import functools

import jax
import jax.numpy as jnp
from jax import lax
from jax.experimental import pallas as pl
from jax.experimental.pallas import tpu as pltpu
from jax.sharding import PartitionSpec as P

F32, BF16 = jnp.float32, jnp.bfloat16
N_Y, N_RING, N_CORE = 4, 8, 2
ROWS, BLOCK, HALF = 512, 512, 256

UP = [
    [(0, 1), (1, 2), (2, 3), (3, 4)],
    [(1, 2), (2, 3), (3, 4), (4, 5)],
    [(2, 3), (3, 4), (4, 5), (5, 6)],
    [(5, 6), (6, 7)],
]
DOWN = [[((3 - a) % 8, (3 - b) % 8) for a, b in step] for step in UP]
CROSS = [
    [(4, 6), (6, 0), (5, 3), (7, 5)],
    [(6, 0), (0, 2), (3, 1), (5, 3)],
]
EARLY = [
    [(0, 0), (5, 1), (6, 2)],
    [(0, 1), (1, 0), (5, 2)],
    [(0, 2), (1, 1), (5, 3)],
    [(0, 3), (1, 2), (2, 1)],
    [(1, 3), (2, 2), (3, 1)],
    [(2, 3), (3, 2), (7, 0)],
    [(3, 3), (6, 0), (7, 1)],
    [(5, 0), (6, 1), (7, 2)],
]
LATE = [
    [(7, 3)], [(6, 3)], [(2, 0)], [(3, 0)], [(8, 0)], [(8, 1)], [(4, 2)], [(4, 3)],
]


def ring_permute(x, pairs):
    full = [
        ((2 * y + a // 4) * 8 + (a % 4) * 2 + c, (2 * y + b // 4) * 8 + (b % 4) * 2 + c)
        for y in range(N_Y)
        for a, b in pairs
        for c in range(N_CORE)
    ]
    return lax.ppermute(x, ("sec", "col"), full)


def swap_cores(x):
    return lax.ppermute(x, "col", [(i, i ^ 1) for i in range(8)])


def split(x):
    hi = x.astype(BF16)
    return hi, (x - hi.astype(F32)).astype(BF16)


def product_kernel(slots, rows, n_bufs, n_second, add, table, *refs):
    bufs, refs = refs[:n_bufs], refs[n_bufs:]
    second, refs = refs[:n_second], refs[n_second:]
    if add:
        base, refs = refs[0], refs[1:]
    out, a_f32, b_f32, l_hi, l_lo, r_hi, r_lo, a_sem, b_sem = refs
    for s in range(slots):
        for b in range(n_bufs):
            @pl.when(table[2 * s] == b)
            def _():
                pltpu.make_async_copy(bufs[b], a_f32.at[s], a_sem.at[s]).start()
        k = table[2 * s + 1]
        for n in range(n_second):
            pltpu.make_async_copy(second[n].at[k], b_f32.at[n, s], b_sem.at[n, s]).start()
    for s in range(slots):
        at = pl.ds(s * HALF, HALF)
        pltpu.make_async_copy(bufs[0], a_f32.at[s], a_sem.at[s]).wait()
        for m in range(2):
            for p in range(2):
                hi, lo = split(a_f32[s, m, :, p * HALF:(p + 1) * HALF])
                l_hi[2 * m + p, :, at] = hi
                l_lo[2 * m + p, :, at] = lo
        for n in range(n_second):
            pltpu.make_async_copy(second[n].at[0], b_f32.at[n, s], b_sem.at[n, s]).wait()
            hi, lo = split(b_f32[n, s])
            r_hi[n, at, :] = hi
            r_lo[n, at, :] = lo
    depth = slots * HALF

    def dots(first, count, n):
        hi = l_hi[first:first + count].reshape(count * rows, depth)
        lo = l_lo[first:first + count].reshape(count * rows, depth)
        dot = functools.partial(jnp.dot, preferred_element_type=F32)
        return dot(hi, r_hi[n]) + dot(lo, r_hi[n]) + dot(hi, r_lo[n])

    def combine(x, y):
        return x[:, :HALF] - y[:, HALF:], x[:, HALF:] + y[:, :HALF]

    def store(m, side, re_im):
        for p in range(2):
            at = (m, slice(None), pl.ds(side * BLOCK + p * HALF, HALF))
            out[at] = re_im[p] + base[at] if add else re_im[p]

    for side in range(n_second // 2):
        both = dots(0, 4, 2 * side)
        store(0, side, combine(both[:rows], both[rows:2 * rows]))
        more = dots(0, 2, 2 * side + 1)
        store(1, side, combine(both[2 * rows:3 * rows] + more[:rows], both[3 * rows:] + more[rows:]))


def products(bufs, second, table, base=None):
    rows, slots = bufs[0].shape[1], table.shape[0] // 2
    n_second = len(second)
    width = n_second // 2 * BLOCK
    operands = [*bufs, *second] + ([] if base is None else [base])
    flops = 2 * 3 * 3 * rows * slots * BLOCK * width
    return pl.pallas_call(
        functools.partial(product_kernel, slots, rows, len(bufs), n_second, base is not None),
        out_shape=jax.ShapeDtypeStruct((2, rows, width), F32),
        grid_spec=pltpu.PrefetchScalarGridSpec(
            num_scalar_prefetch=1,
            grid=(),
            in_specs=[pl.BlockSpec(memory_space=pl.ANY)] * (len(bufs) + n_second)
            + ([] if base is None else [pl.BlockSpec(memory_space=pltpu.VMEM)]),
            out_specs=pl.BlockSpec(memory_space=pltpu.VMEM),
            scratch_shapes=[
                pltpu.VMEM((slots, 2, rows, BLOCK), F32),
                pltpu.VMEM((n_second, slots, HALF, BLOCK), F32),
                pltpu.VMEM((4, rows, slots * HALF), BF16),
                pltpu.VMEM((4, rows, slots * HALF), BF16),
                pltpu.VMEM((n_second, slots * HALF, BLOCK), BF16),
                pltpu.VMEM((n_second, slots * HALF, BLOCK), BF16),
                pltpu.SemaphoreType.DMA((slots,)),
                pltpu.SemaphoreType.DMA((n_second, slots)),
            ],
        ),
        compiler_params=pltpu.CompilerParams(vmem_limit_bytes=44 * 2**20),
        cost_estimate=pl.CostEstimate(flops=flops, bytes_accessed=8 * 2**20, transcendentals=0),
    )(table, *operands)


def shards(pairs):
    own = pairs[0]
    sec, col = lax.axis_index("sec"), lax.axis_index("col")
    upper, core = sec % 2, col % 2
    position = upper * 4 + col // 2

    pieces = [own[:, :HALF], own[:, HALF:]]
    rings = []
    for piece in pieces:
        bufs = {0: piece}
        up = down = piece
        for step in range(4):
            up, down = ring_permute(up, UP[step]), ring_permute(down, DOWN[step])
            bufs[1 + step], bufs[5 + step] = up, down
        rings.append([bufs[i] for i in range(9)])

    low, high = own[:, :HALF], own[:, HALF:]
    kept = jnp.where(core == 0, low, high)
    other = swap_cores(jnp.where(core == 0, high, low))
    second = []
    for mine in (other[0], other[1], kept[0], kept[1]):
        moved = ring_permute(ring_permute(mine, CROSS[0]), CROSS[1])
        second.append(lax.all_gather(jnp.where(upper == 1, mine, moved), "row"))

    early = jnp.array(EARLY, jnp.int32).reshape(8, 6)[position]
    late = jnp.array(LATE, jnp.int32).reshape(8, 2)[position]
    every = jnp.concatenate([early, late])
    first = products(rings[0], second, every)
    last = products(rings[1], second, late, products(rings[1], second, early))
    outs = [part[:, :, BLOCK:] + swap_cores(part[:, :, :BLOCK]) for part in (first, last)]
    return jnp.concatenate(outs, axis=1)[None]


def solution(mesh):
    placed = (P("sec", None, "row", "col"),)
    return jax.shard_map(
        shards, mesh=mesh, in_specs=placed, out_specs=P("sec", None, "row", "col"), check_vma=False
    )
```

time: 426 us -> 319 us (0.75)
  waiting for transfers between devices: 328 us -> 198 us
  starting transfers between devices: 7.78 us -> 56 us
  matrix products: 45.8 us -> 0 us
  Pallas kernels: 0 us -> 37.3 us
  other arithmetic: 29.5 us -> 8.65 us
  local copies, waits for them, and re-layouts: 0.02 us -> 4.55 us
    all_gather x2 -> x4, waiting for transfers between devices: 266 us -> 0.04 us  [shards(): second.append(lax.all_gather(jnp.where(upper == 1, mine, moved), 'row'))]
    ppermute x1 -> x27, waiting for transfers between devices: 61.2 us -> 198 us  [the longest x24 193 us: ring_permute(): return lax.ppermute(x, ('sec', 'col'), full)]
    ppermute x1 -> x27, starting transfers between devices: 7.74 us -> 55.8 us  [the longest x24 52.2 us: ring_permute(): return lax.ppermute(x, ('sec', 'col'), full)]
    dot_general x3 -> x0, matrix products: 45.8 us -> none  [real_dot(): jnp.dot(left, right, precision=lax.Precision.HIGHEST, preferred_element_t...]
    pallas_call x0 -> x3, Pallas kernels: none -> 37.3 us  [products(): pl.pallas_call(functools.partial(product_kernel, slots, rows, len(bufs),...]
    another operation x2 -> x0, other arithmetic: 17.1 us -> none  [real_form(): stacked = jnp.stack([shaped, lower], axis=2)]
    neg x1 -> x0, other arithmetic: 6.51 us -> none  [real_form(): lower = jnp.concatenate([-imag_part, real_part], axis=3)]
  transfers between devices with their start and end apart: 3 -> 31, of which waited for: 3 -> 16; matrix products, arithmetic and copies ran while one was open for 6% -> 2% of each run, Pallas kernels for 0% -> 12%
where the time goes in v1:
time: 319 us; the launch traced here: 318 us
  waiting for transfers between devices  198 us (62%)
  starting transfers between devices  56 us (18%)
  Pallas kernels  37.3 us (12%)
  between operations  13.4 us (4%)
  other arithmetic  8.65 us (3%)
  local copies, waits for them, and re-layouts  4.55 us (1%)
    ppermute x24, waiting for transfers between devices, ring_permute(): return lax.ppermute(x, ('sec', 'col'), full)  193 us
    ppermute x24, starting transfers between devices, ring_permute(): return lax.ppermute(x, ('sec', 'col'), full)  52.2 us
    pallas_call x3, Pallas kernels, products(): pl.pallas_call(functools.partial(product_kernel, slots, rows, len(bufs),...  37.3 us
  transfers between devices with their start and end apart: 31, of which 16 were waited for; matrix products, arithmetic and copies ran while one was open for 2% of the time, Pallas kernels for 12%

profile of v1, /device:TPU:1, one launch (start us, length us, event | category | flops | bytes accessed | tf_op | source)
XLA Modules:
  0.0 318.3 jit_solution(17492389791011833040)
XLA Ops:
  6.5 3.1 fusion
  9.6 0.1 slice_bitcast_fusion
  9.7 1.3 collective-permute-start.15
  11.0 1.3 collective-permute-start.13
  12.3 17.9 %collective-permute-done.15 = f32[256,512]{1,0:T(8,128)} collective-permute-done((f32[256,512]{1,0:T(8,128)S(1)}, f32[256,512]{1,0:T(8,128)}, u32[]{:S(2)}, u32[]{:S(2)}) %collective-permute-start.15) | collective-permute-done | bytes 524320 | tf_op jit(solution)/shard_map/ppermute | solution.py:47
  30.2 1.9 collective-permute-start.16
  32.1 9.3 %collective-permute-done.13 = f32[256,512]{1,0:T(8,128)} collective-permute-done((f32[256,512]{1,0:T(8,128)S(1)}, f32[256,512]{1,0:T(8,128)}, u32[]{:S(2)}, u32[]{:S(2)}) %collective-permute-start.13) | collective-permute-done | bytes 524320 | tf_op jit(solution)/shard_map/ppermute | solution.py:47
  41.5 1.9 collective-permute-start.14
  43.4 9.3 %collective-permute-done.16 = f32[256,512]{1,0:T(8,128)} collective-permute-done((f32[256,512]{1,0:T(8,128)}, f32[256,512]{1,0:T(8,128)}, u32[]{:S(2)}, u32[]{:S(2)}) %collective-permute-start.16) | collective-permute-done | bytes 524320 | tf_op jit(solution)/shard_map/ppermute | solution.py:47
  52.7 11.2 %collective-permute-done.14 = f32[256,512]{1,0:T(8,128)} collective-permute-done((f32[256,512]{1,0:T(8,128)}, f32[256,512]{1,0:T(8,128)}, u32[]{:S(2)}, u32[]{:S(2)}) %collective-permute-start.14) | collective-permute-done | bytes 524320 | tf_op jit(solution)/shard_map/ppermute | solution.py:47
  63.9 2.4 broadcast_select_fusion.2
  66.3 0.0 all-gather.13.cloned.1.call-start
  66.4 0.7 all-gather.13.cloned.1.call-update
  67.1 0.0 all-gather.11.cloned.1.call-start
  67.1 1.3 collective-permute-start.8
  68.5 2.5 collective-permute-done.8
  70.9 0.1 slice_bitcast_fusion.2
  71.0 1.3 collective-permute-start.11
  72.3 1.3 collective-permute-start.9
  73.6 14.5 %collective-permute-done.11 = f32[256,512]{1,0:T(8,128)S(1)} collective-permute-done((f32[256,512]{1,0:T(8,128)S(1)}, f32[256,512]{1,0:T(8,128)S(1)}, u32[]{:S(2)}, u32[]{:S(2)}) %collective-permute-start.11) | collective-permute-done | bytes 524320 | tf_op jit(solution)/shard_map/ppermute | solution.py:47
  88.2 1.9 collective-permute-start.12
  90.1 9.3 %collective-permute-done.9 = f32[256,512]{1,0:T(8,128)S(1)} collective-permute-done((f32[256,512]{1,0:T(8,128)S(1)}, f32[256,512]{1,0:T(8,128)S(1)}, u32[]{:S(2)}, u32[]{:S(2)}) %collective-permute-start.9) | collective-permute-done | bytes 524320 | tf_op jit(solution)/shard_map/ppermute | solution.py:47
  99.4 1.9 collective-permute-start.10
  101.3 9.3 %collective-permute-done.12 = f32[256,512]{1,0:T(8,128)S(1)} collective-permute-done((f32[256,512]{1,0:T(8,128)S(1)}, f32[256,512]{1,0:T(8,128)S(1)}, u32[]{:S(2)}, u32[]{:S(2)}) %collective-permute-start.12) | collective-permute-done | bytes 524320 | tf_op jit(solution)/shard_map/ppermute | solution.py:47
  110.6 11.2 %collective-permute-done.10 = f32[256,512]{1,0:T(8,128)S(1)} collective-permute-done((f32[256,512]{1,0:T(8,128)S(1)}, f32[256,512]{1,0:T(8,128)S(1)}, u32[]{:S(2)}, u32[]{:S(2)}) %collective-permute-start.10) | collective-permute-done | bytes 524320 | tf_op jit(solution)/shard_map/ppermute | solution.py:47
  121.9 1.2 broadcast_select_fusion.4
  123.1 0.0 all-gather.9.cloned.1.call-start
  123.1 1.9 collective-permute-start.4
  125.1 4.3 %collective-permute-start = (f32[2,256,512]{2,1,0:T(8,128)S(1)}, f32[2,256,512]{2,1,0:T(8,128)}, u32[]{:S(2)}, u32[]{:S(2)}) collective-permute-start(f32[2,256,512]{2,1,0:T(8,128)S(1)} %get-tuple-element.5.refs_0_), channel_id=1, source_target_pairs={{0,2},{1,3},{2,4},{3,5},{4,6},{5,7},{6,32},{7,33},{64,66},{65,67},... | collective-permute-start | bytes 3145736 | tf_op jit(solution)/shard_map/ppermute | solution.py:47
  129.4 1.9 collective-permute-start.22
  131.3 4.3 %collective-permute-start.18 = (f32[2,256,512]{2,1,0:T(8,128)S(1)}, f32[2,256,512]{2,1,0:T(8,128)}, u32[]{:S(2)}, u32[]{:S(2)}) collective-permute-start(f32[2,256,512]{2,1,0:T(8,128)S(1)} %get-tuple-element.8.refs_0_), channel_id=1, source_target_pairs={{0,2},{1,3},{2,4},{3,5},{4,6},{5,7},{6,32},{7,33},{64,66},{65,67},... | collective-permute-start | bytes 3145736 | tf_op jit(solution)/shard_map/ppermute | solution.py:47
  135.7 12.9 %collective-permute-done.4.refs_5_ = f32[2,256,512]{2,1,0:T(8,128)} collective-permute-done((f32[2,256,512]{2,1,0:T(8,128)S(1)}, f32[2,256,512]{2,1,0:T(8,128)}, u32[]{:S(2)}, u32[]{:S(2)}) %collective-permute-start.4) | collective-permute-done | bytes 1048608 | tf_op jit(solution)/shard_map/ppermute | solution.py:47
  148.6 3.4 %collective-permute-start.5 = (f32[2,256,512]{2,1,0:T(8,128)}, f32[2,256,512]{2,1,0:T(8,128)}, u32[]{:S(2)}, u32[]{:S(2)}) collective-permute-start(f32[2,256,512]{2,1,0:T(8,128)} %collective-permute-done.4.refs_5_), channel_id=1, source_target_pairs={{4,2},{5,3},{2,0},{3,1},{0,38},{1,39},{38,36},{39,37},{68,66},{69,... | collective-permute-start | bytes 3145736 | tf_op jit(solution)/shard_map/ppermute | solution.py:47
  152.0 1.7 collective-permute-start.1
  153.7 17.3 %collective-permute-done.22.refs_5_ = f32[2,256,512]{2,1,0:T(8,128)S(1)} collective-permute-done((f32[2,256,512]{2,1,0:T(8,128)S(1)}, f32[2,256,512]{2,1,0:T(8,128)S(1)}, u32[]{:S(2)}, u32[]{:S(2)}) %collective-permute-start.22) | collective-permute-done | bytes 1048608 | tf_op jit(solution)/shard_map/ppermute | solution.py:47
  170.9 3.4 %collective-permute-start.23 = (f32[2,256,512]{2,1,0:T(8,128)S(1)}, f32[2,256,512]{2,1,0:T(8,128)}, u32[]{:S(2)}, u32[]{:S(2)}) collective-permute-start(f32[2,256,512]{2,1,0:T(8,128)S(1)} %collective-permute-done.22.refs_5_), channel_id=1, source_target_pairs={{4,2},{5,3},{2,0},{3,1},{0,38},{1,39},{38,36},{39,37},{68,66},{69,... | collective-permute-start | bytes 3145736 | tf_op jit(solution)/shard_map/ppermute | solution.py:47
  174.4 1.6 collective-permute-start.19
  176.0 17.5 %collective-permute-done.5.refs_6_ = f32[2,256,512]{2,1,0:T(8,128)} collective-permute-done((f32[2,256,512]{2,1,0:T(8,128)}, f32[2,256,512]{2,1,0:T(8,128)}, u32[]{:S(2)}, u32[]{:S(2)}) %collective-permute-start.5) | collective-permute-done | bytes 1048608 | tf_op jit(solution)/shard_map/ppermute | solution.py:47
  193.5 3.4 %collective-permute-start.6 = (f32[2,256,512]{2,1,0:T(8,128)}, f32[2,256,512]{2,1,0:T(8,128)}, u32[]{:S(2)}, u32[]{:S(2)}) collective-permute-start(f32[2,256,512]{2,1,0:T(8,128)} %collective-permute-done.5.refs_6_), channel_id=1, source_target_pairs={{2,0},{3,1},{0,38},{1,39},{38,36},{39,37},{36,34},{37,35},{66,64},... | collective-permute-start | bytes 3145736 | tf_op jit(solution)/shard_map/ppermute | solution.py:47
  197.0 1.7 collective-permute-start.2
  198.6 17.4 %collective-permute-done.23.refs_6_ = f32[2,256,512]{2,1,0:T(8,128)} collective-permute-done((f32[2,256,512]{2,1,0:T(8,128)S(1)}, f32[2,256,512]{2,1,0:T(8,128)}, u32[]{:S(2)}, u32[]{:S(2)}) %collective-permute-start.23) | collective-permute-done | bytes 1048608 | tf_op jit(solution)/shard_map/ppermute | solution.py:47
  216.0 3.4 %collective-permute-start.24 = (f32[2,256,512]{2,1,0:T(8,128)}, f32[2,256,512]{2,1,0:T(8,128)}, u32[]{:S(2)}, u32[]{:S(2)}) collective-permute-start(f32[2,256,512]{2,1,0:T(8,128)} %collective-permute-done.23.refs_6_), channel_id=1, source_target_pairs={{2,0},{3,1},{0,38},{1,39},{38,36},{39,37},{36,34},{37,35},{66,64},... | collective-permute-start | bytes 3145736 | tf_op jit(solution)/shard_map/ppermute | solution.py:47
  219.4 1.6 collective-permute-start.20
  221.1 17.4 %collective-permute-done.6.refs_7_ = f32[2,256,512]{2,1,0:T(8,128)} collective-permute-done((f32[2,256,512]{2,1,0:T(8,128)}, f32[2,256,512]{2,1,0:T(8,128)}, u32[]{:S(2)}, u32[]{:S(2)}) %collective-permute-start.6) | collective-permute-done | bytes 1048608 | tf_op jit(solution)/shard_map/ppermute | solution.py:47
  238.5 1.6 collective-permute-start.7
  240.1 1.7 collective-permute-start.3
  241.8 0.7 dynamic-slice_bitcast_fusion.table
  242.5 18.5 %collective-permute-done.24.refs_7_ = f32[2,256,512]{2,1,0:T(8,128)} collective-permute-done((f32[2,256,512]{2,1,0:T(8,128)}, f32[2,256,512]{2,1,0:T(8,128)}, u32[]{:S(2)}, u32[]{:S(2)}) %collective-permute-start.24) | collective-permute-done | bytes 1048608 | tf_op jit(solution)/shard_map/ppermute | solution.py:47
  260.9 1.6 collective-permute-start.25
  262.6 1.6 collective-permute-start.21
  264.2 0.7 dynamic-slice_bitcast_fusion.1.table
  264.9 0.1 pad_add_fusion.table
  265.0 16.5 %shard_map.37 = f32[2,256,1024]{2,1,0:T(8,128)} custom-call(s32[8]{0:T(128)S(1)} %pad_add_fusion.table, f32[2,256,512]{2,1,0:T(8,128)S(1)} %get-tuple-element.5.refs_0_, f32[2,256,512]{2,1,0:T(8,128)} %collective-permute-done.refs_1_, f32[2,256,512]{2,1,0:T(8,128)} %collective-permute-done.1.refs_2_, f32[2,256,512]{2,1,0:T(8,128)} %collective-permute-done.2.refs_3_, ...), custom_call_target="tpu_custom_call" | custom-call | flops 9663676416 | bytes 8388608 | tf_op jit(solution)/shard_map/pallas_call | solution.py:115
  281.5 1.3 slice.49
  282.8 2.2 collective-permute-start.17
  285.0 12.7 %shard_map.38.refs_13_ = f32[2,256,1024]{2,1,0:T(8,128)} custom-call(s32[6]{0:T(128)S(1)} %dynamic-slice_bitcast_fusion.1.table, f32[2,256,512]{2,1,0:T(8,128)S(1)} %get-tuple-element.8.refs_0_, f32[2,256,512]{2,1,0:T(8,128)} %collective-permute-done.18.refs_1_, f32[2,256,512]{2,1,0:T(8,128)} %collective-permute-done.19.refs_2_, ...), custom_call_target="tpu_custom_call" | custom-call | flops 7247757312 | bytes 8388608 | tf_op jit(solution)/shard_map/pallas_call | solution.py:115
  297.7 8.1 %shard_map.39 = f32[2,256,1024]{2,1,0:T(8,128)} custom-call(s32[2]{0:T(128)S(1)} %dynamic-slice_bitcast_fusion.table, f32[2,256,512]{2,1,0:T(8,128)S(1)} %get-tuple-element.8.refs_0_, f32[2,256,512]{2,1,0:T(8,128)} %collective-permute-done.18.refs_1_, f32[2,256,512]{2,1,0:T(8,128)} %collective-permute-done.19.refs_2_, ...), custom_call_target="tpu_custom_call" | custom-call | flops 2415919104 | bytes 8388608 | tf_op jit(solution)/shard_map/pallas_call | solution.py:115
  305.8 1.4 slice.51
  307.3 0.1 collective-permute-start.26
  307.4 0.3 copy-done.1
  307.7 0.2 slice_add_fusion.1
  308.0 2.1 collective-permute-done.26
  310.0 0.2 slice_add_fusion
  310.3 1.5 maximum_bitcast_fusion
  (22 shorter events, 0.1 us)
Async XLA Ops:
  6.5 258.4 %all-gather.15.cloned.1.call-start = ((), (), s32[]{:S(2)}) async-start(), calls=%async_computation.3 | async-start | bytes 2621440 | tf_op jit(solution)/shard_map/all_gather | solution.py:162
  9.7 20.5 %collective-permute-start.15 = (f32[256,512]{1,0:T(8,128)S(1)}, f32[256,512]{1,0:T(8,128)}, u32[]{:S(2)}, u32[]{:S(2)}) collective-permute-start(f32[256,512]{1,0:T(8,128)S(1)} %get-tuple-element.11), channel_id=1, source_target_pairs={{32,36},{33,37},{36,0},{37,1},{34,6},{35,7},{38,34},{39,35},{96,10... | collective-permute-start | bytes 1572872 | tf_op jit(solution)/shard_map/ppermute | solution.py:47
  11.0 30.4 %collective-permute-start.13 = (f32[256,512]{1,0:T(8,128)S(1)}, f32[256,512]{1,0:T(8,128)}, u32[]{:S(2)}, u32[]{:S(2)}) collective-permute-start(f32[256,512]{1,0:T(8,128)S(1)} %get-tuple-element.12), channel_id=1, source_target_pairs={{32,36},{33,37},{36,0},{37,1},{34,6},{35,7},{38,34},{39,35},{96,10... | collective-permute-start | bytes 1572872 | tf_op jit(solution)/shard_map/ppermute | solution.py:47
  30.2 22.5 %collective-permute-start.16 = (f32[256,512]{1,0:T(8,128)}, f32[256,512]{1,0:T(8,128)}, u32[]{:S(2)}, u32[]{:S(2)}) collective-permute-start(f32[256,512]{1,0:T(8,128)} %collective-permute-done.15), channel_id=1, source_target_pairs={{36,0},{37,1},{0,4},{1,5},{6,2},{7,3},{34,6},{35,7},{100,64},{101,... | collective-permute-start | bytes 1572872 | tf_op jit(solution)/shard_map/ppermute | solution.py:47
  41.5 22.5 %collective-permute-start.14 = (f32[256,512]{1,0:T(8,128)}, f32[256,512]{1,0:T(8,128)}, u32[]{:S(2)}, u32[]{:S(2)}) collective-permute-start(f32[256,512]{1,0:T(8,128)} %collective-permute-done.13), channel_id=1, source_target_pairs={{36,0},{37,1},{0,4},{1,5},{6,2},{7,3},{34,6},{35,7},{100,64},{101,... | collective-permute-start | bytes 1572872 | tf_op jit(solution)/shard_map/ppermute | solution.py:47
  66.3 198.6 %all-gather.13.cloned.1.call-start = ((), (), s32[]{:S(2)}) async-start(), calls=%async_computation.2 | async-start | bytes 2621440 | tf_op jit(solution)/shard_map/all_gather | solution.py:162
  67.1 197.9 %all-gather.11.cloned.1.call-start = ((), (), s32[]{:S(2)}) async-start(), calls=%async_computation.1 | async-start | bytes 2621440 | tf_op jit(solution)/shard_map/all_gather | solution.py:162
  67.1 3.8 %collective-permute-start.8 = (f32[2,256,512]{2,1,0:T(8,128)}, f32[2,256,512]{2,1,0:T(8,128)S(1)}, u32[]{:S(2)}, u32[]{:S(2)}) collective-permute-start(f32[2,256,512]{2,1,0:T(8,128)} %get-tuple-element.6), channel_id=1, source_target_pairs={{0,1},{1,0},{2,3},{3,2},{4,5},{5,4},{6,7},{7,6},{8,9},{9,8},{10,11... | collective-permute-start | bytes 3145736 | tf_op jit(solution)/shard_map/ppermute | solution.py:51
  71.0 17.1 %collective-permute-start.11 = (f32[256,512]{1,0:T(8,128)S(1)}, f32[256,512]{1,0:T(8,128)S(1)}, u32[]{:S(2)}, u32[]{:S(2)}) collective-permute-start(f32[256,512]{1,0:T(8,128)S(1)} %get-tuple-element.15), channel_id=1, source_target_pairs={{32,36},{33,37},{36,0},{37,1},{34,6},{35,7},{38,34},{39,35},{96,10... | collective-permute-start | bytes 1572872 | tf_op jit(solution)/shard_map/ppermute | solution.py:47
  72.3 27.1 %collective-permute-start.9 = (f32[256,512]{1,0:T(8,128)S(1)}, f32[256,512]{1,0:T(8,128)S(1)}, u32[]{:S(2)}, u32[]{:S(2)}) collective-permute-start(f32[256,512]{1,0:T(8,128)S(1)} %get-tuple-element.16), channel_id=1, source_target_pairs={{32,36},{33,37},{36,0},{37,1},{34,6},{35,7},{38,34},{39,35},{96,10... | collective-permute-start | bytes 1572872 | tf_op jit(solution)/shard_map/ppermute | solution.py:47
  88.2 22.5 %collective-permute-start.12 = (f32[256,512]{1,0:T(8,128)S(1)}, f32[256,512]{1,0:T(8,128)S(1)}, u32[]{:S(2)}, u32[]{:S(2)}) collective-permute-start(f32[256,512]{1,0:T(8,128)S(1)} %collective-permute-done.11), channel_id=1, source_target_pairs={{36,0},{37,1},{0,4},{1,5},{6,2},{7,3},{34,6},{35,7},{100,64},{101,... | collective-permute-start | bytes 1572872 | tf_op jit(solution)/shard_map/ppermute | solution.py:47
  99.4 22.5 %collective-permute-start.10 = (f32[256,512]{1,0:T(8,128)S(1)}, f32[256,512]{1,0:T(8,128)S(1)}, u32[]{:S(2)}, u32[]{:S(2)}) collective-permute-start(f32[256,512]{1,0:T(8,128)S(1)} %collective-permute-done.9), channel_id=1, source_target_pairs={{36,0},{37,1},{0,4},{1,5},{6,2},{7,3},{34,6},{35,7},{100,64},{101,... | collective-permute-start | bytes 1572872 | tf_op jit(solution)/shard_map/ppermute | solution.py:47
  123.1 142.0 %all-gather.9.cloned.1.call-start = ((), (), s32[]{:S(2)}) async-start(), calls=%async_computation | async-start | bytes 2621440 | tf_op jit(solution)/shard_map/all_gather | solution.py:162
  123.1 25.5 %collective-permute-start.4 = (f32[2,256,512]{2,1,0:T(8,128)S(1)}, f32[2,256,512]{2,1,0:T(8,128)}, u32[]{:S(2)}, u32[]{:S(2)}) collective-permute-start(f32[2,256,512]{2,1,0:T(8,128)S(1)} %get-tuple-element.5.refs_0_), channel_id=1, source_target_pairs={{6,4},{7,5},{4,2},{5,3},{2,0},{3,1},{0,38},{1,39},{70,68},{71,69},... | collective-permute-start | bytes 3145736 | tf_op jit(solution)/shard_map/ppermute | solution.py:47
  125.1 26.9 %collective-permute-start = (f32[2,256,512]{2,1,0:T(8,128)S(1)}, f32[2,256,512]{2,1,0:T(8,128)}, u32[]{:S(2)}, u32[]{:S(2)}) collective-permute-start(f32[2,256,512]{2,1,0:T(8,128)S(1)} %get-tuple-element.5.refs_0_), channel_id=1, source_target_pairs={{0,2},{1,3},{2,4},{3,5},{4,6},{5,7},{6,32},{7,33},{64,66},{65,67},... | collective-permute-start | bytes 3145736 | tf_op jit(solution)/shard_map/ppermute | solution.py:47
  129.4 41.5 %collective-permute-start.22 = (f32[2,256,512]{2,1,0:T(8,128)S(1)}, f32[2,256,512]{2,1,0:T(8,128)S(1)}, u32[]{:S(2)}, u32[]{:S(2)}) collective-permute-start(f32[2,256,512]{2,1,0:T(8,128)S(1)} %get-tuple-element.8.refs_0_), channel_id=1, source_target_pairs={{6,4},{7,5},{4,2},{5,3},{2,0},{3,1},{0,38},{1,39},{70,68},{71,69},... | collective-permute-start | bytes 3145736 | tf_op jit(solution)/shard_map/ppermute | solution.py:47
  131.3 43.1 %collective-permute-start.18 = (f32[2,256,512]{2,1,0:T(8,128)S(1)}, f32[2,256,512]{2,1,0:T(8,128)}, u32[]{:S(2)}, u32[]{:S(2)}) collective-permute-start(f32[2,256,512]{2,1,0:T(8,128)S(1)} %get-tuple-element.8.refs_0_), channel_id=1, source_target_pairs={{0,2},{1,3},{2,4},{3,5},{4,6},{5,7},{6,32},{7,33},{64,66},{65,67},... | collective-permute-start | bytes 3145736 | tf_op jit(solution)/shard_map/ppermute | solution.py:47
  148.6 44.9 %collective-permute-start.5 = (f32[2,256,512]{2,1,0:T(8,128)}, f32[2,256,512]{2,1,0:T(8,128)}, u32[]{:S(2)}, u32[]{:S(2)}) collective-permute-start(f32[2,256,512]{2,1,0:T(8,128)} %collective-permute-done.4.refs_5_), channel_id=1, source_target_pairs={{4,2},{5,3},{2,0},{3,1},{0,38},{1,39},{38,36},{39,37},{68,66},{69,... | collective-permute-start | bytes 3145736 | tf_op jit(solution)/shard_map/ppermute | solution.py:47
  152.0 44.9 %collective-permute-start.1 = (f32[2,256,512]{2,1,0:T(8,128)}, f32[2,256,512]{2,1,0:T(8,128)}, u32[]{:S(2)}, u32[]{:S(2)}) collective-permute-start(f32[2,256,512]{2,1,0:T(8,128)} %collective-permute-done.refs_1_), channel_id=1, source_target_pairs={{2,4},{3,5},{4,6},{5,7},{6,32},{7,33},{32,34},{33,35},{66,68},{67,... | collective-permute-start | bytes 3145736 | tf_op jit(solution)/shard_map/ppermute | solution.py:47
  170.9 45.0 %collective-permute-start.23 = (f32[2,256,512]{2,1,0:T(8,128)S(1)}, f32[2,256,512]{2,1,0:T(8,128)}, u32[]{:S(2)}, u32[]{:S(2)}) collective-permute-start(f32[2,256,512]{2,1,0:T(8,128)S(1)} %collective-permute-done.22.refs_5_), channel_id=1, source_target_pairs={{4,2},{5,3},{2,0},{3,1},{0,38},{1,39},{38,36},{39,37},{68,66},{69,... | collective-permute-start | bytes 3145736 | tf_op jit(solution)/shard_map/ppermute | solution.py:47
  174.4 45.0 %collective-permute-start.19 = (f32[2,256,512]{2,1,0:T(8,128)}, f32[2,256,512]{2,1,0:T(8,128)}, u32[]{:S(2)}, u32[]{:S(2)}) collective-permute-start(f32[2,256,512]{2,1,0:T(8,128)} %collective-permute-done.18.refs_1_), channel_id=1, source_target_pairs={{2,4},{3,5},{4,6},{5,7},{6,32},{7,33},{32,34},{33,35},{66,68},{67,... | collective-permute-start | bytes 3145736 | tf_op jit(solution)/shard_map/ppermute | solution.py:47
  193.5 44.9 %collective-permute-start.6 = (f32[2,256,512]{2,1,0:T(8,128)}, f32[2,256,512]{2,1,0:T(8,128)}, u32[]{:S(2)}, u32[]{:S(2)}) collective-permute-start(f32[2,256,512]{2,1,0:T(8,128)} %collective-permute-done.5.refs_6_), channel_id=1, source_target_pairs={{2,0},{3,1},{0,38},{1,39},{38,36},{39,37},{36,34},{37,35},{66,64},... | collective-permute-start | bytes 3145736 | tf_op jit(solution)/shard_map/ppermute | solution.py:47
  197.0 43.1 %collective-permute-start.2 = (f32[2,256,512]{2,1,0:T(8,128)}, f32[2,256,512]{2,1,0:T(8,128)}, u32[]{:S(2)}, u32[]{:S(2)}) collective-permute-start(f32[2,256,512]{2,1,0:T(8,128)} %collective-permute-done.1.refs_2_), channel_id=1, source_target_pairs={{4,6},{5,7},{6,32},{7,33},{32,34},{33,35},{34,36},{35,37},{68,70},... | collective-permute-start | bytes 3145736 | tf_op jit(solution)/shard_map/ppermute | solution.py:47
  216.0 44.9 %collective-permute-start.24 = (f32[2,256,512]{2,1,0:T(8,128)}, f32[2,256,512]{2,1,0:T(8,128)}, u32[]{:S(2)}, u32[]{:S(2)}) collective-permute-start(f32[2,256,512]{2,1,0:T(8,128)} %collective-permute-done.23.refs_6_), channel_id=1, source_target_pairs={{2,0},{3,1},{0,38},{1,39},{38,36},{39,37},{36,34},{37,35},{66,64},... | collective-permute-start | bytes 3145736 | tf_op jit(solution)/shard_map/ppermute | solution.py:47
  219.4 43.1 %collective-permute-start.20 = (f32[2,256,512]{2,1,0:T(8,128)}, f32[2,256,512]{2,1,0:T(8,128)}, u32[]{:S(2)}, u32[]{:S(2)}) collective-permute-start(f32[2,256,512]{2,1,0:T(8,128)} %collective-permute-done.19.refs_2_), channel_id=1, source_target_pairs={{4,6},{5,7},{6,32},{7,33},{32,34},{33,35},{34,36},{35,37},{68,70},... | collective-permute-start | bytes 3145736 | tf_op jit(solution)/shard_map/ppermute | solution.py:47
  238.5 26.5 %collective-permute-start.7 = (f32[2,256,512]{2,1,0:T(8,128)}, f32[2,256,512]{2,1,0:T(8,128)}, u32[]{:S(2)}, u32[]{:S(2)}) collective-permute-start(f32[2,256,512]{2,1,0:T(8,128)} %collective-permute-done.6.refs_7_), channel_id=1, source_target_pairs={{36,34},{37,35},{34,32},{35,33},{100,98},{101,99},{98,96},{99,97},... | collective-permute-start | bytes 3145736 | tf_op jit(solution)/shard_map/ppermute | solution.py:47
  240.1 24.9 %collective-permute-start.3 = (f32[2,256,512]{2,1,0:T(8,128)}, f32[2,256,512]{2,1,0:T(8,128)}, u32[]{:S(2)}, u32[]{:S(2)}) collective-permute-start(f32[2,256,512]{2,1,0:T(8,128)} %collective-permute-done.2.refs_3_), channel_id=1, source_target_pairs={{34,36},{35,37},{36,38},{37,39},{98,100},{99,101},{100,102},{101,1... | collective-permute-start | bytes 3145736 | tf_op jit(solution)/shard_map/ppermute | solution.py:47
  260.9 24.1 %collective-permute-start.25 = (f32[2,256,512]{2,1,0:T(8,128)}, f32[2,256,512]{2,1,0:T(8,128)}, u32[]{:S(2)}, u32[]{:S(2)}) collective-permute-start(f32[2,256,512]{2,1,0:T(8,128)} %collective-permute-done.24.refs_7_), channel_id=1, source_target_pairs={{36,34},{37,35},{34,32},{35,33},{100,98},{101,99},{98,96},{99,97},... | collective-permute-start | bytes 3145736 | tf_op jit(solution)/shard_map/ppermute | solution.py:47
  262.6 22.4 %collective-permute-start.21 = (f32[2,256,512]{2,1,0:T(8,128)}, f32[2,256,512]{2,1,0:T(8,128)}, u32[]{:S(2)}, u32[]{:S(2)}) collective-permute-start(f32[2,256,512]{2,1,0:T(8,128)} %collective-permute-done.20.refs_3_), channel_id=1, source_target_pairs={{34,36},{35,37},{36,38},{37,39},{98,100},{99,101},{100,102},{101,1... | collective-permute-start | bytes 3145736 | tf_op jit(solution)/shard_map/ppermute | solution.py:47
  282.8 24.6 %collective-permute-start.17 = (f32[2,256,512]{2,1,0:T(8,128)S(1)}, f32[2,256,512]{2,1,0:T(8,128)S(1)}, u32[]{:S(2)}, u32[]{:S(2)}) collective-permute-start(f32[2,256,512]{2,1,0:T(8,128)S(1)} %slice.49), channel_id=1, source_target_pairs={{0,1},{1,0},{2,3},{3,2},{4,5},{5,4},{6,7},{7,6},{8,9},{9,8},{10,11... | collective-permute-start | bytes 3145736 | tf_op jit(solution)/shard_map/ppermute | solution.py:51
  305.8 1.9 copy-start.1
  307.3 2.8 copy-start
  307.3 2.7 collective-permute-start.26
Sparse Core Ops, SparseCore 0:
  66.5 31.8 all-gather.14
  100.2 33.4 all-gather.12
  135.4 33.4 all-gather.10
  170.6 33.4 all-gather.8

commit v2 on v1

v2 whole, which is shorter than its diff:
```python
import functools

import jax
import jax.numpy as jnp
from jax import lax
from jax.experimental import pallas as pl
from jax.experimental.pallas import tpu as pltpu
from jax.sharding import PartitionSpec as P

F32, BF16 = jnp.float32, jnp.bfloat16
N_Y, N_RING, N_CORE = 4, 8, 2
ROWS, BLOCK, HALF = 512, 512, 256

UP = [
    [(0, 1), (1, 2), (2, 3), (3, 4)],
    [(2, 3), (3, 4), (4, 5)],
    [(3, 4), (4, 5), (5, 6)],
    [(5, 6), (6, 7)],
]
LAST = [[(1, 2), (2, 1)], [(2, 3), (1, 0)]]
CROSS = [[(4, 0), (7, 3)], [(5, 1), (6, 2)]]
EARLY = [
    [(0, 0), (5, 1), (6, 2)],
    [(0, 1), (1, 0), (5, 2)],
    [(0, 2), (1, 1), (5, 3)],
    [(0, 3), (1, 2), (2, 1)],
    [(1, 3), (2, 2), (3, 1)],
    [(2, 3), (3, 2), (7, 0)],
    [(3, 3), (6, 0), (7, 1)],
    [(5, 0), (6, 1), (7, 2)],
]
LATE = [[(10, 3)], [(9, 3)], [(9, 0)], [(10, 0)], [(8, 0)], [(8, 1)], [(4, 2)], [(4, 3)]]


def ring_permute(x, pairs):
    full = [
        ((2 * y + a // 4) * 8 + (a % 4) * 2 + c, (2 * y + b // 4) * 8 + (b % 4) * 2 + c)
        for y in range(N_Y)
        for a, b in pairs
        for c in range(N_CORE)
    ]
    return lax.ppermute(x, ("sec", "col"), full)


def mirrored(pairs):
    return [((3 - a) % 8, (3 - b) % 8) for a, b in pairs]


def swap_cores(x):
    return lax.ppermute(x, "col", [(i, i ^ 1) for i in range(8)])


def split(x):
    hi = x.astype(BF16)
    return hi, (x - hi.astype(F32)).astype(BF16)


def product_kernel(slots, rows, n_bufs, layout, add, table, *refs):
    bufs, refs = refs[:n_bufs], refs[n_bufs:]
    n_second = len(layout)
    second = []
    for parts in layout:
        second.append([ref if part is None else ref.at[part] for ref, part in zip(refs, parts)])
        refs = refs[len(parts):]
    if add:
        base, refs = refs[0], refs[1:]
    out, a_f32, b_f32, left, right, a_sem, b_sem = refs
    depth = slots * 3 * HALF
    for s in range(slots):
        for b in range(n_bufs):
            @pl.when(table[2 * s] == b)
            def _():
                pltpu.make_async_copy(bufs[b], a_f32.at[s], a_sem.at[s]).start()
        for n in range(n_second):
            for i in range(4):
                @pl.when(table[2 * s + 1] == i)
                def _():
                    pltpu.make_async_copy(second[n][i], b_f32.at[n, s], b_sem.at[n, s]).start()
    for s in range(slots):
        pltpu.make_async_copy(a_f32.at[s], a_f32.at[s], a_sem.at[s]).wait()
        for m in range(2):
            at = (1 - m) * depth + s * 3 * HALF
            for p in range(2):
                hi, lo = split(a_f32[s, m, :, p * HALF:(p + 1) * HALF])
                for i, part in enumerate((hi, lo, hi)):
                    left[p * rows:(p + 1) * rows, at + i * HALF:at + (i + 1) * HALF] = part
        for n in range(n_second):
            pltpu.make_async_copy(b_f32.at[n, s], b_f32.at[n, s], b_sem.at[n, s]).wait()
            at = n % 2 * depth + s * 3 * HALF
            hi, lo = split(b_f32[n, s])
            for i, part in enumerate((hi, hi, lo)):
                right[n // 2, at + i * HALF:at + (i + 1) * HALF, :] = part

    def combine(x, y):
        return x[:, :HALF] - y[:, HALF:], x[:, HALF:] + y[:, :HALF]

    def store(m, side, re_im):
        for p in range(2):
            at = (m, slice(None), pl.ds(side * BLOCK + p * HALF, HALF))
            out[at] = re_im[p] + base[at] if add else re_im[p]

    for side in range(n_second // 2):
        value = jnp.dot(left[:, depth:], right[side, :depth], preferred_element_type=F32)
        store(0, side, combine(value[:rows], value[rows:]))
        slope = jnp.dot(left[...], right[side], preferred_element_type=F32)
        store(1, side, combine(slope[:rows], slope[rows:]))


def products(bufs, second, table, base=None):
    rows, slots = bufs[0].shape[1], table.shape[0] // 2
    n_second = len(second)
    layout = [[part for _, part in members] for members in second]
    width = n_second // 2 * BLOCK
    operands = [*bufs, *[ref for members in second for ref, _ in members]]
    n_any = len(operands)
    operands += [] if base is None else [base]
    return pl.pallas_call(
        functools.partial(product_kernel, slots, rows, len(bufs), layout, base is not None),
        out_shape=jax.ShapeDtypeStruct((2, rows, width), F32),
        grid_spec=pltpu.PrefetchScalarGridSpec(
            num_scalar_prefetch=1,
            grid=(),
            in_specs=[pl.BlockSpec(memory_space=pl.ANY)] * n_any
            + ([] if base is None else [pl.BlockSpec(memory_space=pltpu.VMEM)]),
            out_specs=pl.BlockSpec(memory_space=pltpu.VMEM),
            scratch_shapes=[
                pltpu.VMEM((slots, 2, rows, BLOCK), F32),
                pltpu.VMEM((n_second, slots, HALF, BLOCK), F32),
                pltpu.VMEM((2 * rows, 6 * slots * HALF), BF16),
                pltpu.VMEM((n_second // 2, 6 * slots * HALF, BLOCK), BF16),
                pltpu.SemaphoreType.DMA((slots,)),
                pltpu.SemaphoreType.DMA((n_second, slots)),
            ],
        ),
        compiler_params=pltpu.CompilerParams(vmem_limit_bytes=62 * 2**20),
        cost_estimate=pl.CostEstimate(flops=1024, bytes_accessed=1024, transcendentals=0),
    )(table, *operands)


def after(x, *earlier):
    return lax.optimization_barrier((x, *earlier))[0]


def shards(pairs):
    own = pairs[0]
    sec, row, col = (lax.axis_index(name) for name in ("sec", "row", "col"))
    upper, core = sec % 2, col % 2
    position = upper * 4 + col // 2

    def across(x, by):
        return lax.ppermute(x, "row", [(i, (i + by) % 4) for i in range(4)])

    def both(x, pairs, *earlier):
        x = tuple(after(part, *earlier) if earlier else part for part in x)
        return ring_permute(x[0], pairs), ring_permute(x[1], mirrored(pairs))

    one = both((own, own), UP[0])
    crossed = ring_permute(own, CROSS[0])
    two = both(one, UP[1], *one, crossed)
    crossed_late = ring_permute(after(own, *one, crossed), CROSS[1])
    three = both(two, UP[2], *two, crossed_late)
    last = after(jnp.where(position == 1, *one), *two, crossed_late)
    last = ring_permute(last, LAST[0])
    inner = (position == 1) | (position == 2)
    mine = jnp.where(upper == 1, own, jnp.where(inner, after(crossed_late, *two), crossed))
    low, high = mine[:, :HALF], mine[:, HALF:]
    kept = jnp.where(core == 0, low, high)
    other = swap_cores(jnp.where(core == 0, high, low))
    near = jnp.stack([other, kept])
    right, left = across(near, 1), across(near, -1)
    four = both(three, UP[3], *three, right, left)
    very_last = ring_permute(after(last, *three, right, left), LAST[1])
    right, left = after(right, *three), after(left, *three)
    far = across(right[0], 1), across(left[1], -1)
    second = [
        [(near, (side, m)), (left, (side, m)), (far[side], m), (right, (side, m))]
        for side in range(2)
        for m in range(2)
    ]
    up, down = zip(one, two, three, four)
    ring = [own, *up, *down, last, very_last]

    def table_of(entries, slots):
        flat = jnp.array(entries, jnp.int32).reshape(8, slots, 2)[position]
        return jnp.stack([flat[:, 0], (flat[:, 1] - row) % 4], axis=1).reshape(-1)

    shifted = [[(b - (b > 4), k) for b, k in entry] for entry in EARLY]
    early, late = table_of(shifted, 3), table_of(LATE, 1)
    early_ring = [ring[i] for i in (0, 1, 2, 3, 5, 6, 7)]
    total = products(ring, second, late, products(early_ring, second, early))
    return (total[:, :, BLOCK:] + swap_cores(total[:, :, :BLOCK]))[None]


def solution(mesh):
    placed = (P("sec", None, "row", "col"),)
    return jax.shard_map(
        shards, mesh=mesh, in_specs=placed, out_specs=P("sec", None, "row", "col"), check_vma=False
    )
```

time: 319 us -> 253 us (0.79); the launches traced: 318 us -> 249 us
  waiting for transfers between devices: 198 us -> 151 us
  between operations: 13.4 us -> 0.81 us
  starting transfers between devices: 56 us -> 47.6 us
    ppermute x24 -> x12, waiting for transfers between devices: 193 us -> 124 us  [ring_permute(): return lax.ppermute(x, ('sec', 'col'), full)]
    ppermute x0 -> x4, waiting for transfers between devices: none -> 23.8 us  [across(): return lax.ppermute(x, 'row', [(i, (i + by) % 4) for i in range(4)])]
    ppermute x24 -> x12, starting transfers between devices: 52.2 us -> 37.7 us  [ring_permute(): return lax.ppermute(x, ('sec', 'col'), full)]
    ppermute x0 -> x4, starting transfers between devices: none -> 5.23 us  [across(): return lax.ppermute(x, 'row', [(i, (i + by) % 4) for i in range(4)])]
    pallas_call x3 -> x2, Pallas kernels: 37.3 us -> 35.3 us  [products(): pl.pallas_call(functools.partial(product_kernel, slots, rows, len(bufs),...]
  transfers between devices with their start and end apart: 31 -> 18, of which waited for: 16 -> 10; matrix products, arithmetic and copies ran while one was open for 2% -> 2% of each run, Pallas kernels for 12% -> 9%
where the time goes in v2:
time: 253 us; the launch traced here: 249 us
  waiting for transfers between devices  151 us (60%)
  starting transfers between devices  47.6 us (19%)
  Pallas kernels  35.3 us (14%)
  other arithmetic  6.93 us (3%)
  local copies, waits for them, and re-layouts  6.77 us (3%)
    ppermute x12, waiting for transfers between devices, ring_permute(): return lax.ppermute(x, ('sec', 'col'), full)  124 us
    ppermute x12, starting transfers between devices, ring_permute(): return lax.ppermute(x, ('sec', 'col'), full)  37.7 us
    pallas_call x2, Pallas kernels, products(): pl.pallas_call(functools.partial(product_kernel, slots, rows, len(bufs),...  35.3 us
    ppermute x4, waiting for transfers between devices, across(): return lax.ppermute(x, 'row', [(i, (i + by) % 4) for i in range(4)])  23.8 us
    ppermute x4, starting transfers between devices, across(): return lax.ppermute(x, 'row', [(i, (i + by) % 4) for i in range(4)])  5.23 us
  transfers between devices with their start and end apart: 18, of which 10 were waited for; matrix products, arithmetic and copies ran while one was open for 2% of the time, Pallas kernels for 9%

profile of v2, /device:TPU:1, one launch (start us, length us, event | category | flops | bytes accessed | tf_op | source)
XLA Modules:
  0.0 248.9 jit_solution(304729085243120216)
XLA Ops:
  0.0 1.3 collective-permute-start.2
  1.3 10.2 %collective-permute-start.1 = (f32[2,512,512]{2,1,0:T(8,128)}, f32[2,512,512]{2,1,0:T(8,128)S(1)}, u32[]{:S(2)}, u32[]{:S(2)}) collective-permute-start(f32[2,512,512]{2,1,0:T(8,128)} %bitcast.21), channel_id=1, source_target_pairs={{6,4},{7,5},{4,2},{5,3},{2,0},{3,1},{0,38},{1,39},{70,68},{71,69},... | collective-permute-start | bytes 6291464 | tf_op jit(solution)/shard_map/ppermute | solution.py:42
  11.5 2.7 %collective-permute-start = (f32[2,512,512]{2,1,0:T(8,128)}, f32[2,512,512]{2,1,0:T(8,128)}, u32[]{:S(2)}, u32[]{:S(2)}) collective-permute-start(f32[2,512,512]{2,1,0:T(8,128)} %bitcast.22), channel_id=1, source_target_pairs={{0,2},{1,3},{2,4},{3,5},{4,6},{5,7},{6,32},{7,33},{64,66},{65,67},... | collective-permute-start | bytes 6291464 | tf_op jit(solution)/shard_map/ppermute | solution.py:42
  14.2 39.2 %collective-permute-done.2 = f32[2,512,512]{2,1,0:T(8,128)S(1)} collective-permute-done((f32[2,512,512]{2,1,0:T(8,128)}, f32[2,512,512]{2,1,0:T(8,128)S(1)}, u32[]{:S(2)}, u32[]{:S(2)}) %collective-permute-start.2) | collective-permute-done | bytes 2097184 | tf_op jit(solution)/shard_map/ppermute | solution.py:42
  53.4 0.0 copy-start.6
  53.4 2.4 collective-permute-done.1.refs_4_.refs_5_
  55.8 0.0 copy-start.3
  55.8 1.3 collective-permute-done.refs_1_
  57.1 0.0 copy-done.6
  57.1 2.0 collective-permute-start.3
  59.1 3.9 %collective-permute-start.4 = (f32[2,512,512]{2,1,0:T(8,128)S(1)}, f32[2,512,512]{2,1,0:T(8,128)}, u32[]{:S(2)}, u32[]{:S(2)}) collective-permute-start(f32[2,512,512]{2,1,0:T(8,128)S(1)} %collective-permute-done.1.refs_4_.refs_5_), channel_id=1, source_target_pairs={{2,0},{3,1},{0,38},{1,39},{38,36},{39,37},{66,64},{67,65},{64,102}... | collective-permute-start | bytes 6291464 | tf_op jit(solution)/shard_map/ppermute | solution.py:42
  63.0 2.0 collective-permute-start.5
  65.0 0.0 collective-permute-done.3.refs_2_
  65.0 41.6 %collective-permute-done.4.refs_5_.refs_6_ = f32[2,512,512]{2,1,0:T(8,128)} collective-permute-done((f32[2,512,512]{2,1,0:T(8,128)S(1)}, f32[2,512,512]{2,1,0:T(8,128)}, u32[]{:S(2)}, u32[]{:S(2)}) %collective-permute-start.4) | collective-permute-done | bytes 2097184 | tf_op jit(solution)/shard_map/ppermute | solution.py:42
  106.6 0.0 collective-permute-done.5
  106.6 3.0 %select_select_fusion = f32[2,512,512]{2,1,0:T(8,128)S(1)} fusion(f32[2,512,512]{2,1,0:T(8,128)} %collective-permute-done.5, f32[2,512,512]{2,1,0:T(8,128)} %copy-done.6, pred[]{:T(512)S(6)} %or.3, pred[]{:T(512)S(6)} %eq.22, f32[1,2,512,512]{3,2,1,0:T(8,128)} %param.3), kind=kLoop, calls=%fused_computation.3 | loop fusion | flops 1048576 | bytes 8388610 | tf_op jit(solution)/shard_map/jit(_where)/select_n | solution.py:165
  109.6 0.2 slice_select_fusion
  109.8 2.8 %collective-permute-start.8 = (f32[2,256,512]{2,1,0:T(8,128)S(1)}, f32[2,256,512]{2,1,0:T(8,128)S(1)}, u32[]{:S(2)}, u32[]{:S(2)}) collective-permute-start(f32[2,256,512]{2,1,0:T(8,128)S(1)} %get-tuple-element.29), channel_id=1, source_target_pairs={{0,1},{1,0},{2,3},{3,2},{4,5},{5,4},{6,7},{7,6},{8,9},{9,8},{10,11... | collective-permute-start | bytes 3145736 | tf_op jit(solution)/shard_map/ppermute | solution.py:50
  112.6 2.0 collective-permute-start.6
  114.5 6.3 %collective-permute-start.7 = (f32[2,512,512]{2,1,0:T(8,128)}, f32[2,512,512]{2,1,0:T(8,128)}, u32[]{:S(2)}, u32[]{:S(2)}) collective-permute-start(f32[2,512,512]{2,1,0:T(8,128)} %collective-permute-done.4.refs_5_.refs_6_), channel_id=1, source_target_pairs={{0,38},{1,39},{38,36},{39,37},{36,34},{37,35},{64,102},{65,103},{1... | collective-permute-start | bytes 6291464 | tf_op jit(solution)/shard_map/ppermute | solution.py:42
  120.9 0.0 collective-permute-done.8
  120.9 0.2 pad_maximum_fusion.refs_7_.refs_11_.refs_15_.refs_19_.refs_23_
  121.0 0.0 copy-start
  121.0 2.6 %collective-permute-start.10 = (f32[2,2,256,512]{3,2,1,0:T(8,128)S(1)}, f32[2,2,256,512]{3,2,1,0:T(8,128)S(1)}, u32[]{:S(2)}, u32[]{:S(2)}) collective-permute-start(f32[2,2,256,512]{3,2,1,0:T(8,128)S(1)} %pad_maximum_fusion.refs_7_.refs_11_.refs_15_.refs_19_.refs_23_), channel_id=1, source_target_pairs={{0,24},{8,0},{16,8},{24,16},{1,25},{9,1},{17,9},{25,17},{2,26},{10... | collective-permute-start | bytes 6291464 | tf_op jit(solution)/shard_map/ppermute | solution.py:151
  123.6 0.0 collective-permute-start.9
  123.6 0.0 copy-done.3
  123.6 0.5 broadcast_select_fusion
  124.1 0.0 copy-done
  124.1 2.1 collective-permute-start.13
  126.2 0.0 collective-permute-done.6.refs_3_
  126.2 38.7 %collective-permute-done.7.refs_6_.refs_7_ = f32[2,512,512]{2,1,0:T(8,128)} collective-permute-done((f32[2,512,512]{2,1,0:T(8,128)}, f32[2,512,512]{2,1,0:T(8,128)}, u32[]{:S(2)}, u32[]{:S(2)}) %collective-permute-start.7) | collective-permute-done | bytes 2097184 | tf_op jit(solution)/shard_map/ppermute | solution.py:42
  164.9 3.4 %collective-permute-done.10.refs_8_.refs_12_.refs_16_.refs_20_.refs_24_ = f32[2,2,256,512]{3,2,1,0:T(8,128)S(1)} collective-permute-done((f32[2,2,256,512]{3,2,1,0:T(8,128)S(1)}, f32[2,2,256,512]{3,2,1,0:T(8,128)S(1)}, u32[]{:S(2)}, u32[]{:S(2)}) %collective-permute-start.10) | collective-permute-done | bytes 2097184 | tf_op jit(solution)/shard_map/ppermute | solution.py:151
  168.3 0.0 copy-start.1
  168.3 3.1 %collective-permute-done.9.refs_10_.refs_14_.refs_18_.refs_22_.refs_26_ = f32[2,2,256,512]{3,2,1,0:T(8,128)S(1)} collective-permute-done((f32[2,2,256,512]{3,2,1,0:T(8,128)S(1)}, f32[2,2,256,512]{3,2,1,0:T(8,128)S(1)}, u32[]{:S(2)}, u32[]{:S(2)}) %collective-permute-start.9) | collective-permute-done | bytes 2097184 | tf_op jit(solution)/shard_map/ppermute | solution.py:151
  171.4 2.0 collective-permute-start.11
  173.4 2.0 collective-permute-start.12
  175.4 0.0 collective-permute-done.13.refs_9_
  175.4 1.3 collective-permute-start.14
  176.7 0.1 slice_bitcast_fusion
  176.8 1.1 slice_bitcast_fusion.1
  177.9 0.0 copy-done.1
  177.9 0.0 copy-done.2
  177.9 0.0 collective-permute-start.15
  177.9 2.7 %collective-permute-start.16 = (f32[2,256,512]{2,1,0:T(8,128)S(1)}, f32[2,256,512]{2,1,0:T(8,128)}, u32[]{:S(2)}, u32[]{:S(2)}) collective-permute-start(f32[2,256,512]{2,1,0:T(8,128)S(1)} %slice_bitcast_fusion), channel_id=1, source_target_pairs={{0,24},{8,0},{16,8},{24,16},{1,25},{9,1},{17,9},{25,17},{2,26},{10... | collective-permute-start | bytes 3145736 | tf_op jit(solution)/shard_map/ppermute | solution.py:151
  180.5 0.7 dynamic-slice_bitcast_fusion.1
  181.2 0.6 fusion.3
  182.5 0.7 dynamic-slice_bitcast_fusion
  183.2 0.1 copy.5
  183.3 0.7 reshape.9.table
  183.9 1.2 add_bitcast_fusion.table
  185.2 17.3 %collective-permute-done.15.refs_9_.refs_13_.refs_17_ = f32[2,256,512]{2,1,0:T(8,128)S(1)} collective-permute-done((f32[2,256,512]{2,1,0:T(8,128)}, f32[2,256,512]{2,1,0:T(8,128)S(1)}, u32[]{:S(2)}, u32[]{:S(2)}) %collective-permute-start.15) | collective-permute-done | bytes 1048608 | tf_op jit(solution)/shard_map/ppermute | solution.py:151
  202.5 0.0 collective-permute-done.16.refs_17_.refs_21_.refs_25_
  202.5 1.0 copy-done.4
  203.5 22.5 %shard_map.37.refs_27_ = f32[2,512,1024]{2,1,0:T(8,128)} custom-call(s32[6]{0:T(128)} %reshape.9.table, f32[2,512,512]{2,1,0:T(8,128)} %bitcast.24, f32[2,512,512]{2,1,0:T(8,128)} %collective-permute-done.refs_1_, f32[2,512,512]{2,1,0:T(8,128)} %collective-permute-done.3.refs_2_, f32[2,512,512]{2,1,0:T(8,128)} %collective-permute-done.6.refs_3_, ...), custom_call_target="tpu_custom_call" | custom-call | flops 1024 | bytes 1024 | tf_op jit(solution)/shard_map/pallas_call | solution.py:117
  226.0 0.0 collective-permute-done.11.refs_4_
  226.0 0.0 collective-permute-done.12.refs_8_
  226.0 0.6 collective-permute-done.14.refs_10_
  226.6 12.8 %shard_map.38 = f32[2,512,1024]{2,1,0:T(8,128)} custom-call(s32[2]{0:T(128)} %add_bitcast_fusion.table, f32[2,512,512]{2,1,0:T(8,128)} %bitcast.25, f32[2,512,512]{2,1,0:T(8,128)} %collective-permute-done.refs_1_, f32[2,512,512]{2,1,0:T(8,128)} %collective-permute-done.3.refs_2_, f32[2,512,512]{2,1,0:T(8,128)} %collective-permute-done.6.refs_3_, ...), custom_call_target="tpu_custom_call" | custom-call | flops 1024 | bytes 1024 | tf_op jit(solution)/shard_map/pallas_call | solution.py:117
  239.4 0.0 copy-start.5
  239.4 1.9 slice.43
  241.3 2.0 collective-permute-start.17
  243.3 3.8 %collective-permute-done.17 = f32[2,512,512]{2,1,0:T(8,128)S(1)} collective-permute-done((f32[2,512,512]{2,1,0:T(8,128)S(1)}, f32[2,512,512]{2,1,0:T(8,128)S(1)}, u32[]{:S(2)}, u32[]{:S(2)}) %collective-permute-start.17) | collective-permute-done | bytes 2097184 | tf_op jit(solution)/shard_map/ppermute | solution.py:50
  247.1 0.0 copy-done.5
  247.1 1.8 fusion
  (4 shorter events, 0.0 us)
Async XLA Ops:
  0.0 53.4 %collective-permute-start.2 = (f32[2,512,512]{2,1,0:T(8,128)}, f32[2,512,512]{2,1,0:T(8,128)S(1)}, u32[]{:S(2)}, u32[]{:S(2)}) collective-permute-start(f32[2,512,512]{2,1,0:T(8,128)} %bitcast.20), channel_id=1, source_target_pairs={{32,0},{33,1},{38,6},{39,7},{96,64},{97,65},{102,70},{103,71},{160... | collective-permute-start | bytes 6291464 | tf_op jit(solution)/shard_map/ppermute | solution.py:42
  1.3 54.5 %collective-permute-start.1 = (f32[2,512,512]{2,1,0:T(8,128)}, f32[2,512,512]{2,1,0:T(8,128)S(1)}, u32[]{:S(2)}, u32[]{:S(2)}) collective-permute-start(f32[2,512,512]{2,1,0:T(8,128)} %bitcast.21), channel_id=1, source_target_pairs={{6,4},{7,5},{4,2},{5,3},{2,0},{3,1},{0,38},{1,39},{70,68},{71,69},... | collective-permute-start | bytes 6291464 | tf_op jit(solution)/shard_map/ppermute | solution.py:42
  11.5 45.6 %collective-permute-start = (f32[2,512,512]{2,1,0:T(8,128)}, f32[2,512,512]{2,1,0:T(8,128)}, u32[]{:S(2)}, u32[]{:S(2)}) collective-permute-start(f32[2,512,512]{2,1,0:T(8,128)} %bitcast.22), channel_id=1, source_target_pairs={{0,2},{1,3},{2,4},{3,5},{4,6},{5,7},{6,32},{7,33},{64,66},{65,67},... | collective-permute-start | bytes 6291464 | tf_op jit(solution)/shard_map/ppermute | solution.py:42
  53.4 3.7 %copy-start.6 = (f32[2,512,512]{2,1,0:T(8,128)}, f32[2,512,512]{2,1,0:T(8,128)S(1)}, u32[]{:S(2)}) copy-start(f32[2,512,512]{2,1,0:T(8,128)S(1)} %collective-permute-done.2) | copy-start | bytes 6291460
  55.8 67.8 %copy-start.3 = (f32[2,512,512]{2,1,0:T(8,128)}, f32[2,512,512]{2,1,0:T(8,128)S(1)}, u32[]{:S(2)}) copy-start(f32[2,512,512]{2,1,0:T(8,128)S(1)} %collective-permute-done.1.refs_4_.refs_5_) | copy-start | bytes 6291460
  57.1 7.9 %collective-permute-start.3 = (f32[2,512,512]{2,1,0:T(8,128)}, f32[2,512,512]{2,1,0:T(8,128)}, u32[]{:S(2)}, u32[]{:S(2)}) collective-permute-start(f32[2,512,512]{2,1,0:T(8,128)} %collective-permute-done.refs_1_), channel_id=1, source_target_pairs={{4,6},{5,7},{6,32},{7,33},{32,34},{33,35},{68,70},{69,71},{70,96},... | collective-permute-start | bytes 6291464 | tf_op jit(solution)/shard_map/ppermute | solution.py:42
  59.1 47.5 %collective-permute-start.4 = (f32[2,512,512]{2,1,0:T(8,128)S(1)}, f32[2,512,512]{2,1,0:T(8,128)}, u32[]{:S(2)}, u32[]{:S(2)}) collective-permute-start(f32[2,512,512]{2,1,0:T(8,128)S(1)} %collective-permute-done.1.refs_4_.refs_5_), channel_id=1, source_target_pairs={{2,0},{3,1},{0,38},{1,39},{38,36},{39,37},{66,64},{67,65},{64,102}... | collective-permute-start | bytes 6291464 | tf_op jit(solution)/shard_map/ppermute | solution.py:42
  63.0 43.6 %collective-permute-start.5 = (f32[2,512,512]{2,1,0:T(8,128)}, f32[2,512,512]{2,1,0:T(8,128)}, u32[]{:S(2)}, u32[]{:S(2)}) collective-permute-start(f32[2,512,512]{2,1,0:T(8,128)} %bitcast.23), channel_id=1, source_target_pairs={{34,2},{35,3},{36,4},{37,5},{98,66},{99,67},{100,68},{101,69},{162... | collective-permute-start | bytes 6291464 | tf_op jit(solution)/shard_map/ppermute | solution.py:42
  109.8 11.0 %collective-permute-start.8 = (f32[2,256,512]{2,1,0:T(8,128)S(1)}, f32[2,256,512]{2,1,0:T(8,128)S(1)}, u32[]{:S(2)}, u32[]{:S(2)}) collective-permute-start(f32[2,256,512]{2,1,0:T(8,128)S(1)} %get-tuple-element.29), channel_id=1, source_target_pairs={{0,1},{1,0},{2,3},{3,2},{4,5},{5,4},{6,7},{7,6},{8,9},{9,8},{10,11... | collective-permute-start | bytes 3145736 | tf_op jit(solution)/shard_map/ppermute | solution.py:50
  112.6 13.6 %collective-permute-start.6 = (f32[2,512,512]{2,1,0:T(8,128)}, f32[2,512,512]{2,1,0:T(8,128)}, u32[]{:S(2)}, u32[]{:S(2)}) collective-permute-start(f32[2,512,512]{2,1,0:T(8,128)} %collective-permute-done.3.refs_2_), channel_id=1, source_target_pairs={{6,32},{7,33},{32,34},{33,35},{34,36},{35,37},{70,96},{71,97},{96,... | collective-permute-start | bytes 6291464 | tf_op jit(solution)/shard_map/ppermute | solution.py:42
  114.5 50.3 %collective-permute-start.7 = (f32[2,512,512]{2,1,0:T(8,128)}, f32[2,512,512]{2,1,0:T(8,128)}, u32[]{:S(2)}, u32[]{:S(2)}) collective-permute-start(f32[2,512,512]{2,1,0:T(8,128)} %collective-permute-done.4.refs_5_.refs_6_), channel_id=1, source_target_pairs={{0,38},{1,39},{38,36},{39,37},{36,34},{37,35},{64,102},{65,103},{1... | collective-permute-start | bytes 6291464 | tf_op jit(solution)/shard_map/ppermute | solution.py:42
  121.0 3.1 %copy-start = (f32[2,2,256,512]{3,2,1,0:T(8,128)}, f32[2,2,256,512]{3,2,1,0:T(8,128)S(1)}, u32[]{:S(2)}) copy-start(f32[2,2,256,512]{3,2,1,0:T(8,128)S(1)} %pad_maximum_fusion.refs_7_.refs_11_.refs_15_.refs_19_.refs_23_) | copy-start | bytes 6291460
  121.0 47.3 %collective-permute-start.10 = (f32[2,2,256,512]{3,2,1,0:T(8,128)S(1)}, f32[2,2,256,512]{3,2,1,0:T(8,128)S(1)}, u32[]{:S(2)}, u32[]{:S(2)}) collective-permute-start(f32[2,2,256,512]{3,2,1,0:T(8,128)S(1)} %pad_maximum_fusion.refs_7_.refs_11_.refs_15_.refs_19_.refs_23_), channel_id=1, source_target_pairs={{0,24},{8,0},{16,8},{24,16},{1,25},{9,1},{17,9},{25,17},{2,26},{10... | collective-permute-start | bytes 6291464 | tf_op jit(solution)/shard_map/ppermute | solution.py:151
  123.6 47.8 %collective-permute-start.9 = (f32[2,2,256,512]{3,2,1,0:T(8,128)S(1)}, f32[2,2,256,512]{3,2,1,0:T(8,128)S(1)}, u32[]{:S(2)}, u32[]{:S(2)}) collective-permute-start(f32[2,2,256,512]{3,2,1,0:T(8,128)S(1)} %pad_maximum_fusion.refs_7_.refs_11_.refs_15_.refs_19_.refs_23_), channel_id=1, source_target_pairs={{0,8},{8,16},{16,24},{24,0},{1,9},{9,17},{17,25},{25,1},{2,10},{10... | collective-permute-start | bytes 6291464 | tf_op jit(solution)/shard_map/ppermute | solution.py:151
  124.1 51.3 %collective-permute-start.13 = (f32[2,512,512]{2,1,0:T(8,128)S(1)}, f32[2,512,512]{2,1,0:T(8,128)}, u32[]{:S(2)}, u32[]{:S(2)}) collective-permute-start(f32[2,512,512]{2,1,0:T(8,128)S(1)} %broadcast_select_fusion), channel_id=1, source_target_pairs={{2,4},{3,5},{4,2},{5,3},{66,68},{67,69},{68,66},{69,67},{130,132},... | collective-permute-start | bytes 6291464 | tf_op jit(solution)/shard_map/ppermute | solution.py:42
  168.3 9.5 %copy-start.1 = (f32[2,2,256,512]{3,2,1,0:T(8,128)}, f32[2,2,256,512]{3,2,1,0:T(8,128)S(1)}, u32[]{:S(2)}) copy-start(f32[2,2,256,512]{3,2,1,0:T(8,128)S(1)} %collective-permute-done.10.refs_8_.refs_12_.refs_16_.refs_20_.refs_24_) | copy-start | bytes 6291460
  171.4 6.5 %copy-start.2 = (f32[2,2,256,512]{3,2,1,0:T(8,128)}, f32[2,2,256,512]{3,2,1,0:T(8,128)S(1)}, u32[]{:S(2)}) copy-start(f32[2,2,256,512]{3,2,1,0:T(8,128)S(1)} %collective-permute-done.9.refs_10_.refs_14_.refs_18_.refs_22_.refs_26_) | copy-start | bytes 6291460
  171.4 54.6 %collective-permute-start.11 = (f32[2,512,512]{2,1,0:T(8,128)}, f32[2,512,512]{2,1,0:T(8,128)}, u32[]{:S(2)}, u32[]{:S(2)}) collective-permute-start(f32[2,512,512]{2,1,0:T(8,128)} %collective-permute-done.6.refs_3_), channel_id=1, source_target_pairs={{34,36},{35,37},{36,38},{37,39},{98,100},{99,101},{100,102},{101,1... | collective-permute-start | bytes 6291464 | tf_op jit(solution)/shard_map/ppermute | solution.py:42
  173.4 52.6 %collective-permute-start.12 = (f32[2,512,512]{2,1,0:T(8,128)}, f32[2,512,512]{2,1,0:T(8,128)}, u32[]{:S(2)}, u32[]{:S(2)}) collective-permute-start(f32[2,512,512]{2,1,0:T(8,128)} %collective-permute-done.7.refs_6_.refs_7_), channel_id=1, source_target_pairs={{36,34},{37,35},{34,32},{35,33},{100,98},{101,99},{98,96},{99,97},... | collective-permute-start | bytes 6291464 | tf_op jit(solution)/shard_map/ppermute | solution.py:42
  175.4 51.2 %collective-permute-start.14 = (f32[2,512,512]{2,1,0:T(8,128)}, f32[2,512,512]{2,1,0:T(8,128)}, u32[]{:S(2)}, u32[]{:S(2)}) collective-permute-start(f32[2,512,512]{2,1,0:T(8,128)} %collective-permute-done.13.refs_9_), channel_id=1, source_target_pairs={{4,6},{5,7},{2,0},{3,1},{68,70},{69,71},{66,64},{67,65},{132,134},... | collective-permute-start | bytes 6291464 | tf_op jit(solution)/shard_map/ppermute | solution.py:42
  177.9 24.6 %collective-permute-start.15 = (f32[2,256,512]{2,1,0:T(8,128)}, f32[2,256,512]{2,1,0:T(8,128)S(1)}, u32[]{:S(2)}, u32[]{:S(2)}) collective-permute-start(f32[2,256,512]{2,1,0:T(8,128)} %slice_bitcast_fusion.1), channel_id=1, source_target_pairs={{0,8},{8,16},{16,24},{24,0},{1,9},{9,17},{17,25},{25,1},{2,10},{10... | collective-permute-start | bytes 3145736 | tf_op jit(solution)/shard_map/ppermute | solution.py:151
  177.9 24.6 %collective-permute-start.16 = (f32[2,256,512]{2,1,0:T(8,128)S(1)}, f32[2,256,512]{2,1,0:T(8,128)}, u32[]{:S(2)}, u32[]{:S(2)}) collective-permute-start(f32[2,256,512]{2,1,0:T(8,128)S(1)} %slice_bitcast_fusion), channel_id=1, source_target_pairs={{0,24},{8,0},{16,8},{24,16},{1,25},{9,1},{17,9},{25,17},{2,26},{10... | collective-permute-start | bytes 3145736 | tf_op jit(solution)/shard_map/ppermute | solution.py:151
  202.5 1.0 copy-start.4
  239.4 7.7 %copy-start.5 = (f32[2,512,1024]{2,1,0:T(8,128)S(1)}, f32[2,512,1024]{2,1,0:T(8,128)}, u32[]{:S(2)}) copy-start(f32[2,512,1024]{2,1,0:T(8,128)} %shard_map.38) | copy-start | bytes 12582916
  241.3 5.7 %collective-permute-start.17 = (f32[2,512,512]{2,1,0:T(8,128)S(1)}, f32[2,512,512]{2,1,0:T(8,128)S(1)}, u32[]{:S(2)}, u32[]{:S(2)}) collective-permute-start(f32[2,512,512]{2,1,0:T(8,128)S(1)} %slice.43), channel_id=1, source_target_pairs={{0,1},{1,0},{2,3},{3,2},{4,5},{5,4},{6,7},{7,6},{8,9},{9,8},{10,11... | collective-permute-start | bytes 6291464 | tf_op jit(solution)/shard_map/ppermute | solution.py:50

commit v3 on v2

--- a/solution.py
+++ b/solution.py
@@ -63,8 +63,9 @@
         second.append([ref if part is None else ref.at[part] for ref, part in zip(refs, parts)])
         refs = refs[len(parts):]
     if add:
-        base, refs = refs[0], refs[1:]
-    out, a_f32, b_f32, left, right, a_sem, b_sem = refs
+        base, refs = refs[:n_second // 2], refs[n_second // 2:]
+    outs, refs = refs[:n_second // 2], refs[n_second // 2:]
+    a_f32, b_f32, left, right, a_sem, b_sem = refs
     depth = slots * 3 * HALF
     for s in range(slots):
         for b in range(n_bufs):
@@ -72,7 +73,7 @@
             def _():
                 pltpu.make_async_copy(bufs[b], a_f32.at[s], a_sem.at[s]).start()
         for n in range(n_second):
-            for i in range(4):
+            for i in range(len(second[n])):
                 @pl.when(table[2 * s + 1] == i)
                 def _():
                     pltpu.make_async_copy(second[n][i], b_f32.at[n, s], b_sem.at[n, s]).start()
@@ -96,8 +97,8 @@
 
     def store(m, side, re_im):
         for p in range(2):
-            at = (m, slice(None), pl.ds(side * BLOCK + p * HALF, HALF))
-            out[at] = re_im[p] + base[at] if add else re_im[p]
+            at = (m, slice(None), slice(p * HALF, (p + 1) * HALF))
+            outs[side][at] = re_im[p] + base[side][at] if add else re_im[p]
 
     for side in range(n_second // 2):
         value = jnp.dot(left[:, depth:], right[side, :depth], preferred_element_type=F32)
@@ -110,19 +111,19 @@
     rows, slots = bufs[0].shape[1], table.shape[0] // 2
     n_second = len(second)
     layout = [[part for _, part in members] for members in second]
-    width = n_second // 2 * BLOCK
+    sides = n_second // 2
     operands = [*bufs, *[ref for members in second for ref, _ in members]]
     n_any = len(operands)
-    operands += [] if base is None else [base]
+    operands += [] if base is None else base
     return pl.pallas_call(
         functools.partial(product_kernel, slots, rows, len(bufs), layout, base is not None),
-        out_shape=jax.ShapeDtypeStruct((2, rows, width), F32),
+        out_shape=[jax.ShapeDtypeStruct((2, rows, BLOCK), F32)] * sides,
         grid_spec=pltpu.PrefetchScalarGridSpec(
             num_scalar_prefetch=1,
             grid=(),
             in_specs=[pl.BlockSpec(memory_space=pl.ANY)] * n_any
-            + ([] if base is None else [pl.BlockSpec(memory_space=pltpu.VMEM)]),
-            out_specs=pl.BlockSpec(memory_space=pltpu.VMEM),
+            + [pl.BlockSpec(memory_space=pltpu.VMEM)] * (len(operands) - n_any),
+            out_specs=[pl.BlockSpec(memory_space=pltpu.VMEM)] * sides,
             scratch_shapes=[
                 pltpu.VMEM((slots, 2, rows, BLOCK), F32),
                 pltpu.VMEM((n_second, slots, HALF, BLOCK), F32),
@@ -155,18 +156,17 @@
         return ring_permute(x[0], pairs), ring_permute(x[1], mirrored(pairs))
 
     one = both((own, own), UP[0])
-    crossed = ring_permute(own, CROSS[0])
+    low, high = own[:, :HALF], own[:, HALF:]
+    kept = jnp.where(core == 0, low, high)
+    near = jnp.stack([swap_cores(jnp.where(core == 0, high, low)), kept])
+    crossed = ring_permute(near, CROSS[0])
     two = both(one, UP[1], *one, crossed)
-    crossed_late = ring_permute(after(own, *one, crossed), CROSS[1])
+    crossed_late = ring_permute(after(near, *one, crossed), CROSS[1])
     three = both(two, UP[2], *two, crossed_late)
     last = after(jnp.where(position == 1, *one), *two, crossed_late)
     last = ring_permute(last, LAST[0])
     inner = (position == 1) | (position == 2)
-    mine = jnp.where(upper == 1, own, jnp.where(inner, after(crossed_late, *two), crossed))
-    low, high = mine[:, :HALF], mine[:, HALF:]
-    kept = jnp.where(core == 0, low, high)
-    other = swap_cores(jnp.where(core == 0, high, low))
-    near = jnp.stack([other, kept])
+    near = jnp.where(upper == 1, near, jnp.where(inner, after(crossed_late, *two), crossed))
     right, left = across(near, 1), across(near, -1)
     four = both(three, UP[3], *three, right, left)
     very_last = ring_permute(after(last, *three, right, left), LAST[1])
@@ -180,15 +180,29 @@
     up, down = zip(one, two, three, four)
     ring = [own, *up, *down, last, very_last]
 
-    def table_of(entries, slots):
-        flat = jnp.array(entries, jnp.int32).reshape(8, slots, 2)[position]
-        return jnp.stack([flat[:, 0], (flat[:, 1] - row) % 4], axis=1).reshape(-1)
-
-    shifted = [[(b - (b > 4), k) for b, k in entry] for entry in EARLY]
-    early, late = table_of(shifted, 3), table_of(LATE, 1)
-    early_ring = [ring[i] for i in (0, 1, 2, 3, 5, 6, 7)]
-    total = products(ring, second, late, products(early_ring, second, early))
-    return (total[:, :, BLOCK:] + swap_cores(total[:, :, :BLOCK]))[None]
+    def table_of(slots, bufs, members):
+        rows = [
+            [
+                [(bufs.index(b), members.index((k - r) % 4)) for b, k in slots(EARLY[p], LATE[p], r)]
+                for r in range(4)
+            ]
+            for p in range(N_RING)
+        ]
+        return jnp.array(rows, jnp.int32).reshape(N_RING, 4, -1)[position, row]
+
+    def ordered(early, r):
+        return sorted(early, key=lambda slot: (slot[1] - r) % 4 == 2)
+
+    early_bufs, late_bufs = (0, 1, 2, 3, 5, 6, 7), (4, 8, 9, 10)
+    early_ring, late_ring = [ring[i] for i in early_bufs], [ring[i] for i in late_bufs]
+    close = [[members[i] for i in (0, 1, 3)] for members in second]
+    first = table_of(lambda early, late, r: ordered(early, r)[:2], early_bufs, (0, 1, 3))
+    third = table_of(lambda early, late, r: ordered(early, r)[2:], early_bufs, (0, 1, 2, 3))
+    final = table_of(lambda early, late, r: late, late_bufs, (0, 1, 2, 3))
+    total = products(early_ring, close, first)
+    total = products(early_ring, second, third, total)
+    total = products(late_ring, second, final, total)
+    return (total[1] + swap_cores(total[0]))[None]
 
 
 def solution(mesh):

time: 253 us -> 244 us (0.964)
  waiting for transfers between devices: 151 us -> 142 us
  Pallas kernels: 35.3 us -> 42.1 us
  starting transfers between devices: 47.6 us -> 40.8 us
  other arithmetic: 6.93 us -> 9.95 us
    ppermute x12, waiting for transfers between devices: 124 us -> 104 us  [ring_permute(): return lax.ppermute(x, ('sec', 'col'), full)]
    ppermute x4, waiting for transfers between devices: 23.8 us -> 34.6 us  [across(): return lax.ppermute(x, 'row', [(i, (i + by) % 4) for i in range(4)])]
    ppermute x12, starting transfers between devices: 37.7 us -> 27.8 us  [ring_permute(): return lax.ppermute(x, ('sec', 'col'), full)]
    pallas_call x2 -> x3, Pallas kernels: 35.3 us -> 42.1 us  [products(): pl.pallas_call(functools.partial(product_kernel, slots, rows, len(bufs),...]
    ppermute x2, starting transfers between devices: 4.71 us -> 7.61 us  [swap_cores(): return lax.ppermute(x, 'col', [(i, i ^ 1) for i in range(8)])]
  transfers between devices with their start and end apart: 18 -> 18, of which waited for: 10 -> 8; matrix products, arithmetic and copies ran while one was open for 2% -> 4% of each run, Pallas kernels for 9% -> 12%
where the time goes in v3:
time: 244 us; the launch traced here: 242 us
  waiting for transfers between devices  142 us (58%)
  Pallas kernels  42.1 us (17%)
  starting transfers between devices  40.8 us (17%)
  other arithmetic  9.95 us (4%)
  local copies, waits for them, and re-layouts  6.9 us (3%)
    ppermute x12, waiting for transfers between devices, ring_permute(): return lax.ppermute(x, ('sec', 'col'), full)  104 us
    pallas_call x3, Pallas kernels, products(): pl.pallas_call(functools.partial(product_kernel, slots, rows, len(bufs),...  42.1 us
    ppermute x4, waiting for transfers between devices, across(): return lax.ppermute(x, 'row', [(i, (i + by) % 4) for i in range(4)])  34.6 us
    ppermute x12, starting transfers between devices, ring_permute(): return lax.ppermute(x, ('sec', 'col'), full)  27.8 us
    ppermute x2, starting transfers between devices, swap_cores(): return lax.ppermute(x, 'col', [(i, i ^ 1) for i in range(8)])  7.61 us
    ppermute x4, starting transfers between devices, across(): return lax.ppermute(x, 'row', [(i, (i + by) % 4) for i in range(4)])  5.43 us
  transfers between devices with their start and end apart: 18, of which 8 were waited for; matrix products, arithmetic and copies ran while one was open for 4% of the time, Pallas kernels for 12%

profile of v3, /device:TPU:1, one launch (start us, length us, event | category | flops | bytes accessed | tf_op | source)
XLA Modules:
  0.0 242.3 jit_solution(4187490886589042231)
XLA Ops:
  0.0 0.0 copy-start.4
  0.0 1.9 slice_select_fusion
  1.9 3.3 %collective-permute-start.2 = (f32[2,256,512]{2,1,0:T(8,128)S(1)}, f32[2,256,512]{2,1,0:T(8,128)S(1)}, u32[]{:S(2)}, u32[]{:S(2)}) collective-permute-start(f32[2,256,512]{2,1,0:T(8,128)S(1)} %get-tuple-element.41), channel_id=1, source_target_pairs={{0,1},{1,0},{2,3},{3,2},{4,5},{5,4},{6,7},{7,6},{8,9},{9,8},{10,11... | collective-permute-start | bytes 3145736 | tf_op jit(solution)/shard_map/ppermute | solution.py:50
  5.3 0.0 copy-done.4
  5.3 1.9 collective-permute-start
  7.2 4.6 %collective-permute-start.1 = (f32[2,512,512]{2,1,0:T(8,128)S(1)}, f32[2,512,512]{2,1,0:T(8,128)}, u32[]{:S(2)}, u32[]{:S(2)}) collective-permute-start(f32[2,512,512]{2,1,0:T(8,128)S(1)} %bitcast.20), channel_id=1, source_target_pairs={{6,4},{7,5},{4,2},{5,3},{2,0},{3,1},{0,38},{1,39},{70,68},{71,69},... | collective-permute-start | bytes 6291464 | tf_op jit(solution)/shard_map/ppermute | solution.py:42
  11.8 0.0 collective-permute-done.2
  11.8 0.0 copy-start.6
  11.8 1.7 pad_maximum_fusion
  13.5 0.0 copy-done.6
  13.5 1.3 collective-permute-start.3
  14.8 37.1 %collective-permute-done.refs_1_ = f32[2,512,512]{2,1,0:T(8,128)S(1)} collective-permute-done((f32[2,512,512]{2,1,0:T(8,128)S(1)}, f32[2,512,512]{2,1,0:T(8,128)S(1)}, u32[]{:S(2)}, u32[]{:S(2)}) %collective-permute-start) | collective-permute-done | bytes 2097184 | tf_op jit(solution)/shard_map/ppermute | solution.py:42
  51.9 0.0 copy-start.3
  51.9 4.7 %collective-permute-done.1.refs_4_ = f32[2,512,512]{2,1,0:T(8,128)} collective-permute-done((f32[2,512,512]{2,1,0:T(8,128)S(1)}, f32[2,512,512]{2,1,0:T(8,128)}, u32[]{:S(2)}, u32[]{:S(2)}) %collective-permute-start.1) | collective-permute-done | bytes 2097184 | tf_op jit(solution)/shard_map/ppermute | solution.py:42
  56.6 9.6 %collective-permute-done.3 = f32[2,2,256,512]{3,2,1,0:T(8,128)S(1)} collective-permute-done((f32[2,2,256,512]{3,2,1,0:T(8,128)}, f32[2,2,256,512]{3,2,1,0:T(8,128)S(1)}, u32[]{:S(2)}, u32[]{:S(2)}) %collective-permute-start.3) | collective-permute-done | bytes 2097184 | tf_op jit(solution)/shard_map/ppermute | solution.py:42
  66.2 2.0 collective-permute-start.6
  68.2 0.0 copy-done.8
  68.2 1.9 collective-permute-start.5
  70.1 2.0 collective-permute-start.4
  72.1 2.2 broadcast_select_fusion
  74.4 0.0 copy-done.3
  74.4 0.0 collective-permute-done.6
  74.4 41.7 %collective-permute-done.5.refs_5_ = f32[2,512,512]{2,1,0:T(8,128)} collective-permute-done((f32[2,512,512]{2,1,0:T(8,128)}, f32[2,512,512]{2,1,0:T(8,128)}, u32[]{:S(2)}, u32[]{:S(2)}) %collective-permute-start.5) | collective-permute-done | bytes 2097184 | tf_op jit(solution)/shard_map/ppermute | solution.py:42
  116.1 0.0 collective-permute-done.4.refs_2_
  116.1 0.0 copy-done.7
  116.1 0.0 copy-done.9
  116.1 0.8 select_select_fusion.refs_7_.refs_10_.refs_13_.refs_16_.refs_11_.refs_15_.refs_19_.refs_4_.refs_8_.refs_12_
  116.9 0.0 copy-start
  116.9 1.3 collective-permute-start.9
  118.2 1.5 collective-permute-start.10
  119.7 4.8 %collective-permute-start.8 = (f32[2,512,512]{2,1,0:T(8,128)}, f32[2,512,512]{2,1,0:T(8,128)}, u32[]{:S(2)}, u32[]{:S(2)}) collective-permute-start(f32[2,512,512]{2,1,0:T(8,128)} %collective-permute-done.5.refs_5_), channel_id=1, source_target_pairs={{0,38},{1,39},{38,36},{39,37},{36,34},{37,35},{64,102},{65,103},{1... | collective-permute-start | bytes 6291464 | tf_op jit(solution)/shard_map/ppermute | solution.py:42
  124.4 2.0 collective-permute-start.7
  126.4 2.0 collective-permute-start.13
  128.4 34.6 %collective-permute-done.9.refs_9_.refs_12_.refs_15_.refs_18_.refs_10_.refs_14_.refs_22_.refs_7_.refs_11_.refs_19_ = f32[2,2,256,512]{3,2,1,0:T(8,128)S(1)} collective-permute-done((f32[2,2,256,512]{3,2,1,0:T(8,128)S(1)}, f32[2,2,256,512]{3,2,1,0:T(8,128)S(1)}, u32[]{:S(2)}, u32[]{:S(2)}) %collective-permute-start.9) | collective-permute-done | bytes 2097184 | tf_op jit(solution)/shard_map/ppermute | solution.py:152
  163.0 2.6 %collective-permute-done.8.refs_6_ = f32[2,512,512]{2,1,0:T(8,128)} collective-permute-done((f32[2,512,512]{2,1,0:T(8,128)}, f32[2,512,512]{2,1,0:T(8,128)}, u32[]{:S(2)}, u32[]{:S(2)}) %collective-permute-start.8) | collective-permute-done | bytes 2097184 | tf_op jit(solution)/shard_map/ppermute | solution.py:42
  165.6 0.0 collective-permute-done.7.refs_3_
  165.6 0.0 collective-permute-done.10.refs_8_.refs_11_.refs_14_.refs_17_.refs_12_.refs_16_.refs_20_.refs_5_.refs_9_.refs_13_
  165.6 0.0 collective-permute-done.13.refs_2_
  165.6 1.3 collective-permute-start.14
  166.9 2.0 collective-permute-start.12
  169.0 2.0 collective-permute-start.11
  170.9 1.1 slice_bitcast_fusion.1
  172.0 0.0 collective-permute-start.15
  172.0 0.0 copy-done.2
  172.0 1.1 slice_bitcast_fusion
  173.1 0.0 copy-done
  173.1 0.0 copy-done.1
  173.1 2.7 %collective-permute-start.16 = (f32[2,256,512]{2,1,0:T(8,128)}, f32[2,256,512]{2,1,0:T(8,128)}, u32[]{:S(2)}, u32[]{:S(2)}) collective-permute-start(f32[2,256,512]{2,1,0:T(8,128)} %slice_bitcast_fusion), channel_id=1, source_target_pairs={{0,24},{8,0},{16,8},{24,16},{1,25},{9,1},{17,9},{25,17},{2,26},{10... | collective-permute-start | bytes 3145736 | tf_op jit(solution)/shard_map/ppermute | solution.py:152
  175.8 1.3 fusion.2.table
  177.1 1.2 fusion.1.table
  178.3 1.2 fusion.table
  179.5 16.5 %shard_map.46 = (f32[2,512,512]{2,1,0:T(8,128)}, f32[2,512,512]{2,1,0:T(8,128)}) custom-call(s32[4]{0:T(128)} %fusion.2.table, f32[2,512,512]{2,1,0:T(8,128)} %bitcast.17, f32[2,512,512]{2,1,0:T(8,128)} %copy-done.3, f32[2,512,512]{2,1,0:T(8,128)} %collective-permute-done.4.refs_2_, f32[2,512,512]{2,1,0:T(8,128)} %collective-permute-done.7.refs_3_, ...), custom_call_target="tpu_custom_call" | custom-call | flops 1024 | bytes 1024 | tf_op jit(solution)/shard_map/pallas_call | solution.py:118
  196.0 0.0 collective-permute-done.15.refs_9_.refs_13_.refs_6_.refs_10_
  196.0 0.0 copy-start.5
  196.0 0.0 collective-permute-done.16.refs_17_.refs_21_.refs_14_.refs_18_
  196.0 0.9 copy-done.5
  197.0 12.7 %shard_map.47 = (f32[2,512,512]{2,1,0:T(8,128)}, f32[2,512,512]{2,1,0:T(8,128)}) custom-call(s32[2]{0:T(128)} %fusion.1.table, f32[2,512,512]{2,1,0:T(8,128)} %bitcast.18, f32[2,512,512]{2,1,0:T(8,128)} %copy-done.3, f32[2,512,512]{2,1,0:T(8,128)} %collective-permute-done.4.refs_2_, f32[2,512,512]{2,1,0:T(8,128)} %collective-permute-done.7.refs_3_, ...), custom_call_target="tpu_custom_call" | custom-call | flops 1024 | bytes 1024 | tf_op jit(solution)/shard_map/pallas_call | solution.py:118
  209.7 8.1 %collective-permute-done.14.refs_3_ = f32[2,512,512]{2,1,0:T(8,128)} collective-permute-done((f32[2,512,512]{2,1,0:T(8,128)}, f32[2,512,512]{2,1,0:T(8,128)}, u32[]{:S(2)}, u32[]{:S(2)}) %collective-permute-start.14) | collective-permute-done | bytes 2097184 | tf_op jit(solution)/shard_map/ppermute | solution.py:42
  217.8 0.0 collective-permute-done.12.refs_1_
  217.8 0.0 collective-permute-done.11.refs_0_
  217.8 12.9 %shard_map.48 = (f32[2,512,512]{2,1,0:T(8,128)}, f32[2,512,512]{2,1,0:T(8,128)}) custom-call(s32[2]{0:T(128)} %fusion.table, f32[2,512,512]{2,1,0:T(8,128)} %collective-permute-done.11.refs_0_, f32[2,512,512]{2,1,0:T(8,128)} %collective-permute-done.12.refs_1_, f32[2,512,512]{2,1,0:T(8,128)} %collective-permute-done.13.refs_2_, ...), custom_call_target="tpu_custom_call" | custom-call | flops 1024 | bytes 1024 | tf_op jit(solution)/shard_map/pallas_call | solution.py:118
  230.7 4.3 %collective-permute-start.17 = (f32[2,512,512]{2,1,0:T(8,128)}, f32[2,512,512]{2,1,0:T(8,128)S(1)}, u32[]{:S(2)}, u32[]{:S(2)}) collective-permute-start(f32[2,512,512]{2,1,0:T(8,128)} %get-tuple-element.40), channel_id=1, source_target_pairs={{0,1},{1,0},{2,3},{3,2},{4,5},{5,4},{6,7},{7,6},{8,9},{9,8},{10,11... | collective-permute-start | bytes 6291464 | tf_op jit(solution)/shard_map/ppermute | solution.py:50
  235.0 4.0 %collective-permute-done.17 = f32[2,512,512]{2,1,0:T(8,128)S(1)} collective-permute-done((f32[2,512,512]{2,1,0:T(8,128)}, f32[2,512,512]{2,1,0:T(8,128)S(1)}, u32[]{:S(2)}, u32[]{:S(2)}) %collective-permute-start.17) | collective-permute-done | bytes 2097184 | tf_op jit(solution)/shard_map/ppermute | solution.py:50
  239.0 3.4 %add_bitcast_fusion = f32[1,2,512,512]{3,2,1,0:T(8,128)} fusion(f32[2,512,512]{2,1,0:T(8,128)} %get-tuple-element.39, f32[2,512,512]{2,1,0:T(8,128)S(1)} %collective-permute-done.17), kind=kLoop, calls=%fused_computation.1 | loop fusion | flops 524288 | bytes 6291456 | tf_op jit(solution)/shard_map/broadcast_in_dim | solution.py:205
  (5 shorter events, 0.0 us)
Async XLA Ops:
  0.0 5.3 %copy-start.4 = (f32[1,2,512,512]{3,2,1,0:T(8,128)S(1)}, f32[1,2,512,512]{3,2,1,0:T(8,128)}, u32[]{:S(2)}) copy-start(f32[1,2,512,512]{3,2,1,0:T(8,128)} %param.4) | copy-start | bytes 6291460
  1.9 9.9 %collective-permute-start.2 = (f32[2,256,512]{2,1,0:T(8,128)S(1)}, f32[2,256,512]{2,1,0:T(8,128)S(1)}, u32[]{:S(2)}, u32[]{:S(2)}) collective-permute-start(f32[2,256,512]{2,1,0:T(8,128)S(1)} %get-tuple-element.41), channel_id=1, source_target_pairs={{0,1},{1,0},{2,3},{3,2},{4,5},{5,4},{6,7},{7,6},{8,9},{9,8},{10,11... | collective-permute-start | bytes 3145736 | tf_op jit(solution)/shard_map/ppermute | solution.py:50
  5.3 46.6 %collective-permute-start = (f32[2,512,512]{2,1,0:T(8,128)S(1)}, f32[2,512,512]{2,1,0:T(8,128)S(1)}, u32[]{:S(2)}, u32[]{:S(2)}) collective-permute-start(f32[2,512,512]{2,1,0:T(8,128)S(1)} %bitcast.19), channel_id=1, source_target_pairs={{0,2},{1,3},{2,4},{3,5},{4,6},{5,7},{6,32},{7,33},{64,66},{65,67},... | collective-permute-start | bytes 6291464 | tf_op jit(solution)/shard_map/ppermute | solution.py:42
  7.2 49.4 %collective-permute-start.1 = (f32[2,512,512]{2,1,0:T(8,128)S(1)}, f32[2,512,512]{2,1,0:T(8,128)}, u32[]{:S(2)}, u32[]{:S(2)}) collective-permute-start(f32[2,512,512]{2,1,0:T(8,128)S(1)} %bitcast.20), channel_id=1, source_target_pairs={{6,4},{7,5},{4,2},{5,3},{2,0},{3,1},{0,38},{1,39},{70,68},{71,69},... | collective-permute-start | bytes 6291464 | tf_op jit(solution)/shard_map/ppermute | solution.py:42
  11.8 1.7 copy-start.6
  13.5 52.7 %collective-permute-start.3 = (f32[2,2,256,512]{3,2,1,0:T(8,128)}, f32[2,2,256,512]{3,2,1,0:T(8,128)S(1)}, u32[]{:S(2)}, u32[]{:S(2)}) collective-permute-start(f32[2,2,256,512]{3,2,1,0:T(8,128)} %pad_maximum_fusion), channel_id=1, source_target_pairs={{32,0},{33,1},{38,6},{39,7},{96,64},{97,65},{102,70},{103,71},{160... | collective-permute-start | bytes 6291464 | tf_op jit(solution)/shard_map/ppermute | solution.py:42
  51.9 22.5 %copy-start.3 = (f32[2,512,512]{2,1,0:T(8,128)}, f32[2,512,512]{2,1,0:T(8,128)S(1)}, u32[]{:S(2)}) copy-start(f32[2,512,512]{2,1,0:T(8,128)S(1)} %collective-permute-done.refs_1_) | copy-start | bytes 6291460
  66.2 2.0 copy-start.8
  66.2 8.2 %collective-permute-start.6 = (f32[2,2,256,512]{3,2,1,0:T(8,128)}, f32[2,2,256,512]{3,2,1,0:T(8,128)}, u32[]{:S(2)}, u32[]{:S(2)}) collective-permute-start(f32[2,2,256,512]{3,2,1,0:T(8,128)} %pad_maximum_fusion), channel_id=1, source_target_pairs={{34,2},{35,3},{36,4},{37,5},{98,66},{99,67},{100,68},{101,69},{162... | collective-permute-start | bytes 6291464 | tf_op jit(solution)/shard_map/ppermute | solution.py:42
  68.2 47.9 %collective-permute-start.5 = (f32[2,512,512]{2,1,0:T(8,128)}, f32[2,512,512]{2,1,0:T(8,128)}, u32[]{:S(2)}, u32[]{:S(2)}) collective-permute-start(f32[2,512,512]{2,1,0:T(8,128)} %collective-permute-done.1.refs_4_), channel_id=1, source_target_pairs={{2,0},{3,1},{0,38},{1,39},{38,36},{39,37},{66,64},{67,65},{64,102}... | collective-permute-start | bytes 6291464 | tf_op jit(solution)/shard_map/ppermute | solution.py:42
  70.1 46.0 %collective-permute-start.4 = (f32[2,512,512]{2,1,0:T(8,128)S(1)}, f32[2,512,512]{2,1,0:T(8,128)}, u32[]{:S(2)}, u32[]{:S(2)}) collective-permute-start(f32[2,512,512]{2,1,0:T(8,128)S(1)} %collective-permute-done.refs_1_), channel_id=1, source_target_pairs={{4,6},{5,7},{6,32},{7,33},{32,34},{33,35},{68,70},{69,71},{70,96},... | collective-permute-start | bytes 6291464 | tf_op jit(solution)/shard_map/ppermute | solution.py:42
  72.1 44.0 %copy-start.7 = (f32[2,256,512]{2,1,0:T(8,128)S(1)}, f32[2,256,512]{2,1,0:T(8,128)}, u32[]{:S(2)}) copy-start(f32[2,256,512]{2,1,0:T(8,128)} %copy-done.6) | copy-start | bytes 3145732
  72.1 44.0 %copy-start.9 = (f32[2,2,256,512]{3,2,1,0:T(8,128)S(1)}, f32[2,2,256,512]{3,2,1,0:T(8,128)}, u32[]{:S(2)}) copy-start(f32[2,2,256,512]{3,2,1,0:T(8,128)} %copy-done.8) | copy-start | bytes 6291460
  116.9 56.2 %copy-start = (f32[2,2,256,512]{3,2,1,0:T(8,128)}, f32[2,2,256,512]{3,2,1,0:T(8,128)S(1)}, u32[]{:S(2)}) copy-start(f32[2,2,256,512]{3,2,1,0:T(8,128)S(1)} %select_select_fusion.refs_7_.refs_10_.refs_13_.refs_16_.refs_11_.refs_15_.refs_19_.refs_4_.refs_8_.refs_12_) | copy-start | bytes 6291460
  116.9 46.1 %collective-permute-start.9 = (f32[2,2,256,512]{3,2,1,0:T(8,128)S(1)}, f32[2,2,256,512]{3,2,1,0:T(8,128)S(1)}, u32[]{:S(2)}, u32[]{:S(2)}) collective-permute-start(f32[2,2,256,512]{3,2,1,0:T(8,128)S(1)} %select_select_fusion.refs_7_.refs_10_.refs_13_.refs_16_.refs_11_.refs_15_.refs_19_.refs_4_.refs_8_.refs_12_), channel_id=1, source_target_pairs={{0,8},{8,16},{16,24},{24,0},{1,9},{9,17},{17,25},{25,1},{2,10},{10... | collective-permute-start | bytes 6291464 | tf_op jit(solution)/shard_map/ppermute | solution.py:152
  118.2 47.4 %collective-permute-start.10 = (f32[2,2,256,512]{3,2,1,0:T(8,128)S(1)}, f32[2,2,256,512]{3,2,1,0:T(8,128)S(1)}, u32[]{:S(2)}, u32[]{:S(2)}) collective-permute-start(f32[2,2,256,512]{3,2,1,0:T(8,128)S(1)} %select_select_fusion.refs_7_.refs_10_.refs_13_.refs_16_.refs_11_.refs_15_.refs_19_.refs_4_.refs_8_.refs_12_), channel_id=1, source_target_pairs={{0,24},{8,0},{16,8},{24,16},{1,25},{9,1},{17,9},{25,17},{2,26},{10... | collective-permute-start | bytes 6291464 | tf_op jit(solution)/shard_map/ppermute | solution.py:152
  119.7 45.9 %collective-permute-start.8 = (f32[2,512,512]{2,1,0:T(8,128)}, f32[2,512,512]{2,1,0:T(8,128)}, u32[]{:S(2)}, u32[]{:S(2)}) collective-permute-start(f32[2,512,512]{2,1,0:T(8,128)} %collective-permute-done.5.refs_5_), channel_id=1, source_target_pairs={{0,38},{1,39},{38,36},{39,37},{36,34},{37,35},{64,102},{65,103},{1... | collective-permute-start | bytes 6291464 | tf_op jit(solution)/shard_map/ppermute | solution.py:42
  124.4 41.2 %collective-permute-start.7 = (f32[2,512,512]{2,1,0:T(8,128)}, f32[2,512,512]{2,1,0:T(8,128)}, u32[]{:S(2)}, u32[]{:S(2)}) collective-permute-start(f32[2,512,512]{2,1,0:T(8,128)} %collective-permute-done.4.refs_2_), channel_id=1, source_target_pairs={{6,32},{7,33},{32,34},{33,35},{34,36},{35,37},{70,96},{71,97},{96,... | collective-permute-start | bytes 6291464 | tf_op jit(solution)/shard_map/ppermute | solution.py:42
  126.4 39.2 %collective-permute-start.13 = (f32[2,512,512]{2,1,0:T(8,128)S(1)}, f32[2,512,512]{2,1,0:T(8,128)}, u32[]{:S(2)}, u32[]{:S(2)}) collective-permute-start(f32[2,512,512]{2,1,0:T(8,128)S(1)} %broadcast_select_fusion), channel_id=1, source_target_pairs={{2,4},{3,5},{4,2},{5,3},{66,68},{67,69},{68,66},{69,67},{130,132},... | collective-permute-start | bytes 6291464 | tf_op jit(solution)/shard_map/ppermute | solution.py:42
  163.0 10.1 %copy-start.1 = (f32[2,2,256,512]{3,2,1,0:T(8,128)}, f32[2,2,256,512]{3,2,1,0:T(8,128)S(1)}, u32[]{:S(2)}) copy-start(f32[2,2,256,512]{3,2,1,0:T(8,128)S(1)} %collective-permute-done.9.refs_9_.refs_12_.refs_15_.refs_18_.refs_10_.refs_14_.refs_22_.refs_7_.refs_11_.refs_19_) | copy-start | bytes 6291460
  165.6 6.4 %copy-start.2 = (f32[2,2,256,512]{3,2,1,0:T(8,128)}, f32[2,2,256,512]{3,2,1,0:T(8,128)S(1)}, u32[]{:S(2)}) copy-start(f32[2,2,256,512]{3,2,1,0:T(8,128)S(1)} %collective-permute-done.10.refs_8_.refs_11_.refs_14_.refs_17_.refs_12_.refs_16_.refs_20_.refs_5_.refs_9_.refs_13_) | copy-start | bytes 6291460
  165.6 52.1 %collective-permute-start.14 = (f32[2,512,512]{2,1,0:T(8,128)}, f32[2,512,512]{2,1,0:T(8,128)}, u32[]{:S(2)}, u32[]{:S(2)}) collective-permute-start(f32[2,512,512]{2,1,0:T(8,128)} %collective-permute-done.13.refs_2_), channel_id=1, source_target_pairs={{4,6},{5,7},{2,0},{3,1},{68,70},{69,71},{66,64},{67,65},{132,134},... | collective-permute-start | bytes 6291464 | tf_op jit(solution)/shard_map/ppermute | solution.py:42
  166.9 50.9 %collective-permute-start.12 = (f32[2,512,512]{2,1,0:T(8,128)}, f32[2,512,512]{2,1,0:T(8,128)}, u32[]{:S(2)}, u32[]{:S(2)}) collective-permute-start(f32[2,512,512]{2,1,0:T(8,128)} %collective-permute-done.8.refs_6_), channel_id=1, source_target_pairs={{36,34},{37,35},{34,32},{35,33},{100,98},{101,99},{98,96},{99,97},... | collective-permute-start | bytes 6291464 | tf_op jit(solution)/shard_map/ppermute | solution.py:42
  169.0 48.8 %collective-permute-start.11 = (f32[2,512,512]{2,1,0:T(8,128)}, f32[2,512,512]{2,1,0:T(8,128)}, u32[]{:S(2)}, u32[]{:S(2)}) collective-permute-start(f32[2,512,512]{2,1,0:T(8,128)} %collective-permute-done.7.refs_3_), channel_id=1, source_target_pairs={{34,36},{35,37},{36,38},{37,39},{98,100},{99,101},{100,102},{101,1... | collective-permute-start | bytes 6291464 | tf_op jit(solution)/shard_map/ppermute | solution.py:42
  172.0 24.0 %collective-permute-start.15 = (f32[2,256,512]{2,1,0:T(8,128)}, f32[2,256,512]{2,1,0:T(8,128)S(1)}, u32[]{:S(2)}, u32[]{:S(2)}) collective-permute-start(f32[2,256,512]{2,1,0:T(8,128)} %slice_bitcast_fusion.1), channel_id=1, source_target_pairs={{0,8},{8,16},{16,24},{24,0},{1,9},{9,17},{17,25},{25,1},{2,10},{10... | collective-permute-start | bytes 3145736 | tf_op jit(solution)/shard_map/ppermute | solution.py:152
  173.1 22.9 %collective-permute-start.16 = (f32[2,256,512]{2,1,0:T(8,128)}, f32[2,256,512]{2,1,0:T(8,128)}, u32[]{:S(2)}, u32[]{:S(2)}) collective-permute-start(f32[2,256,512]{2,1,0:T(8,128)} %slice_bitcast_fusion), channel_id=1, source_target_pairs={{0,24},{8,0},{16,8},{24,16},{1,25},{9,1},{17,9},{25,17},{2,26},{10... | collective-permute-start | bytes 3145736 | tf_op jit(solution)/shard_map/ppermute | solution.py:152
  196.0 1.0 copy-start.5
  230.7 8.3 %collective-permute-start.17 = (f32[2,512,512]{2,1,0:T(8,128)}, f32[2,512,512]{2,1,0:T(8,128)S(1)}, u32[]{:S(2)}, u32[]{:S(2)}) collective-permute-start(f32[2,512,512]{2,1,0:T(8,128)} %get-tuple-element.40), channel_id=1, source_target_pairs={{0,1},{1,0},{2,3},{3,2},{4,5},{5,4},{6,7},{7,6},{8,9},{9,8},{10,11... | collective-permute-start | bytes 6291464 | tf_op jit(solution)/shard_map/ppermute | solution.py:50

commit v4 on v3

--- a/solution.py
+++ b/solution.py
@@ -160,16 +160,16 @@
     kept = jnp.where(core == 0, low, high)
     near = jnp.stack([swap_cores(jnp.where(core == 0, high, low)), kept])
     crossed = ring_permute(near, CROSS[0])
-    two = both(one, UP[1], *one, crossed)
+    two = both(one, UP[1], *one)
     crossed_late = ring_permute(after(near, *one, crossed), CROSS[1])
-    three = both(two, UP[2], *two, crossed_late)
+    three = both(two, UP[2], *two)
     last = after(jnp.where(position == 1, *one), *two, crossed_late)
     last = ring_permute(last, LAST[0])
     inner = (position == 1) | (position == 2)
     near = jnp.where(upper == 1, near, jnp.where(inner, after(crossed_late, *two), crossed))
     right, left = across(near, 1), across(near, -1)
-    four = both(three, UP[3], *three, right, left)
-    very_last = ring_permute(after(last, *three, right, left), LAST[1])
+    four = both(three, UP[3], *three)
+    very_last = ring_permute(after(last, *three), LAST[1])
     right, left = after(right, *three), after(left, *three)
     far = across(right[0], 1), across(left[1], -1)
     second = [

time: 244 us -> 235 us (0.963)
  waiting for transfers between devices: 142 us -> 126 us
  starting transfers between devices: 40.8 us -> 46 us
  other arithmetic: 9.95 us -> 12.9 us
    ppermute x4, waiting for transfers between devices: 34.6 us -> 9.04 us  [across(): return lax.ppermute(x, 'row', [(i, (i + by) % 4) for i in range(4)])]
    ppermute x12, waiting for transfers between devices: 104 us -> 113 us  [ring_permute(): return lax.ppermute(x, ('sec', 'col'), full)]
    ppermute x12, starting transfers between devices: 27.8 us -> 33.2 us  [ring_permute(): return lax.ppermute(x, ('sec', 'col'), full)]
  transfers between devices with their start and end apart: 18 -> 18, of which waited for: 8 -> 7; matrix products, arithmetic and copies ran while one was open for 4% -> 6% of each run, Pallas kernels for 12% -> 12%
where the time goes in v4:
time: 235 us; the launch traced here: 234 us
  waiting for transfers between devices  126 us (54%)
  starting transfers between devices  46 us (20%)
  Pallas kernels  42.2 us (18%)
  other arithmetic  12.9 us (5%)
  local copies, waits for them, and re-layouts  6.9 us (3%)
    ppermute x12, waiting for transfers between devices, ring_permute(): return lax.ppermute(x, ('sec', 'col'), full)  113 us
    pallas_call x3, Pallas kernels, products(): pl.pallas_call(functools.partial(product_kernel, slots, rows, len(bufs),...  42.2 us
    ppermute x12, starting transfers between devices, ring_permute(): return lax.ppermute(x, ('sec', 'col'), full)  33.2 us
    ppermute x4, waiting for transfers between devices, across(): return lax.ppermute(x, 'row', [(i, (i + by) % 4) for i in range(4)])  9.04 us
    ppermute x2, starting transfers between devices, swap_cores(): return lax.ppermute(x, 'col', [(i, i ^ 1) for i in range(8)])  7.15 us
    ppermute x4, starting transfers between devices, across(): return lax.ppermute(x, 'row', [(i, (i + by) % 4) for i in range(4)])  5.62 us
  transfers between devices with their start and end apart: 18, of which 7 were waited for; matrix products, arithmetic and copies ran while one was open for 6% of the time, Pallas kernels for 12%

profile of v4, /device:TPU:1, one launch (start us, length us, event | category | flops | bytes accessed | tf_op | source)
XLA Modules:
  0.0 234.4 jit_solution(18076828411212131970)
XLA Ops:
  0.0 0.0 copy-start.4
  0.0 1.9 slice_select_fusion
  1.9 3.3 %collective-permute-start.8 = (f32[2,256,512]{2,1,0:T(8,128)S(1)}, f32[2,256,512]{2,1,0:T(8,128)S(1)}, u32[]{:S(2)}, u32[]{:S(2)}) collective-permute-start(f32[2,256,512]{2,1,0:T(8,128)S(1)} %get-tuple-element.41), channel_id=1, source_target_pairs={{0,1},{1,0},{2,3},{3,2},{4,5},{5,4},{6,7},{7,6},{8,9},{9,8},{10,11... | collective-permute-start | bytes 3145736 | tf_op jit(solution)/shard_map/ppermute | solution.py:50
  5.3 0.0 copy-done.4
  5.3 1.9 collective-permute-start
  7.2 4.6 %collective-permute-start.1 = (f32[2,512,512]{2,1,0:T(8,128)S(1)}, f32[2,512,512]{2,1,0:T(8,128)}, u32[]{:S(2)}, u32[]{:S(2)}) collective-permute-start(f32[2,512,512]{2,1,0:T(8,128)S(1)} %bitcast.20), channel_id=1, source_target_pairs={{6,4},{7,5},{4,2},{5,3},{2,0},{3,1},{0,38},{1,39},{70,68},{71,69},... | collective-permute-start | bytes 6291464 | tf_op jit(solution)/shard_map/ppermute | solution.py:42
  11.8 0.0 collective-permute-done.8
  11.8 0.0 copy-start.6
  11.8 1.6 pad_maximum_fusion
  13.4 0.0 copy-done.6
  13.4 1.3 collective-permute-start.9
  14.7 37.1 %collective-permute-done.refs_1_ = f32[2,512,512]{2,1,0:T(8,128)S(1)} collective-permute-done((f32[2,512,512]{2,1,0:T(8,128)S(1)}, f32[2,512,512]{2,1,0:T(8,128)S(1)}, u32[]{:S(2)}, u32[]{:S(2)}) %collective-permute-start) | collective-permute-done | bytes 2097184 | tf_op jit(solution)/shard_map/ppermute | solution.py:42
  51.9 0.0 copy-start.3
  51.9 4.7 %collective-permute-done.1.refs_4_ = f32[2,512,512]{2,1,0:T(8,128)} collective-permute-done((f32[2,512,512]{2,1,0:T(8,128)S(1)}, f32[2,512,512]{2,1,0:T(8,128)}, u32[]{:S(2)}, u32[]{:S(2)}) %collective-permute-start.1) | collective-permute-done | bytes 2097184 | tf_op jit(solution)/shard_map/ppermute | solution.py:42
  56.6 2.0 collective-permute-start.2
  58.7 5.4 %collective-permute-start.3 = (f32[2,512,512]{2,1,0:T(8,128)}, f32[2,512,512]{2,1,0:T(8,128)}, u32[]{:S(2)}, u32[]{:S(2)}) collective-permute-start(f32[2,512,512]{2,1,0:T(8,128)} %collective-permute-done.1.refs_4_), channel_id=1, source_target_pairs={{2,0},{3,1},{0,38},{1,39},{38,36},{39,37},{66,64},{67,65},{64,102}... | collective-permute-start | bytes 6291464 | tf_op jit(solution)/shard_map/ppermute | solution.py:42
  64.1 2.2 collective-permute-done.9
  66.3 2.0 collective-permute-start.10
  68.2 0.0 collective-permute-done.2.refs_2_
  68.2 40.0 %collective-permute-done.3.refs_5_ = f32[2,512,512]{2,1,0:T(8,128)} collective-permute-done((f32[2,512,512]{2,1,0:T(8,128)}, f32[2,512,512]{2,1,0:T(8,128)}, u32[]{:S(2)}, u32[]{:S(2)}) %collective-permute-start.3) | collective-permute-done | bytes 2097184 | tf_op jit(solution)/shard_map/ppermute | solution.py:42
  108.3 6.7 %collective-permute-start.5 = (f32[2,512,512]{2,1,0:T(8,128)}, f32[2,512,512]{2,1,0:T(8,128)}, u32[]{:S(2)}, u32[]{:S(2)}) collective-permute-start(f32[2,512,512]{2,1,0:T(8,128)} %collective-permute-done.3.refs_5_), channel_id=1, source_target_pairs={{0,38},{1,39},{38,36},{39,37},{36,34},{37,35},{64,102},{65,103},{1... | collective-permute-start | bytes 6291464 | tf_op jit(solution)/shard_map/ppermute | solution.py:42
  115.0 2.0 collective-permute-start.4
  117.0 3.4 %broadcast_select_fusion = f32[2,512,512]{2,1,0:T(8,128)} fusion(f32[2,512,512]{2,1,0:T(8,128)S(1)} %collective-permute-done.refs_1_, f32[2,512,512]{2,1,0:T(8,128)} %collective-permute-done.1.refs_4_, pred[]{:T(512)S(6)} %eq.17), kind=kLoop, calls=%fused_computation.6 | loop fusion | flops 524288 | bytes 6291457 | tf_op jit(solution)/shard_map/jit(_where)/select_n | solution.py:166
  120.4 0.0 copy-done.3
  120.4 0.0 collective-permute-done.10
  120.4 2.0 collective-permute-start.11
  122.4 2.6 %select_select_fusion.refs_7_.refs_10_.refs_13_.refs_16_.refs_11_.refs_15_.refs_19_.refs_4_.refs_8_.refs_12_ = f32[2,2,256,512]{3,2,1,0:T(8,128)S(1)} fusion(f32[2,2,256,512]{3,2,1,0:T(8,128)} %collective-permute-done.10, f32[2,2,256,512]{3,2,1,0:T(8,128)} %collective-permute-done.9, pred[]{:T(512)S(6)} %or.3, pred[]{:T(512)S(6)} %eq.19, ...), kind=kLoop, calls=%fused_computation.2 | loop fusion | flops 1572864 | bytes 8388610 | tf_op jit(solution)/shard_map/jit(_where)/select_n | solution.py:169
  125.0 0.0 copy-start
  125.0 1.3 collective-permute-start.14
  126.3 1.5 collective-permute-start.13
  127.8 29.1 %collective-permute-done.5.refs_6_ = f32[2,512,512]{2,1,0:T(8,128)} collective-permute-done((f32[2,512,512]{2,1,0:T(8,128)}, f32[2,512,512]{2,1,0:T(8,128)}, u32[]{:S(2)}, u32[]{:S(2)}) %collective-permute-start.5) | collective-permute-done | bytes 2097184 | tf_op jit(solution)/shard_map/ppermute | solution.py:42
  156.9 0.0 collective-permute-done.4.refs_3_
  156.9 2.0 collective-permute-start.7
  158.9 2.0 collective-permute-start.6
  160.9 0.0 collective-permute-done.11.refs_2_
  160.9 1.3 collective-permute-start.12
  162.2 9.0 %collective-permute-done.14.refs_9_.refs_12_.refs_15_.refs_18_.refs_10_.refs_14_.refs_22_.refs_7_.refs_11_.refs_19_ = f32[2,2,256,512]{3,2,1,0:T(8,128)S(1)} collective-permute-done((f32[2,2,256,512]{3,2,1,0:T(8,128)S(1)}, f32[2,2,256,512]{3,2,1,0:T(8,128)S(1)}, u32[]{:S(2)}, u32[]{:S(2)}) %collective-permute-start.14) | collective-permute-done | bytes 2097184 | tf_op jit(solution)/shard_map/ppermute | solution.py:152
  171.2 0.0 copy-start.1
  171.2 0.0 collective-permute-done.13.refs_8_.refs_11_.refs_14_.refs_17_.refs_12_.refs_16_.refs_20_.refs_5_.refs_9_.refs_13_
  171.2 0.0 copy-start.2
  171.2 1.2 slice_bitcast_fusion.1
  172.4 1.0 collective-permute-start.15
  173.4 0.0 copy-done.2
  173.4 1.1 slice_bitcast_fusion
  174.5 0.0 copy-done
  174.5 0.0 copy-done.1
  174.5 1.8 collective-permute-start.16
  176.4 1.2 fusion.2.table
  177.6 1.2 fusion.1.table
  178.8 1.2 fusion.table
  180.0 16.5 %shard_map.46 = (f32[2,512,512]{2,1,0:T(8,128)}, f32[2,512,512]{2,1,0:T(8,128)}) custom-call(s32[4]{0:T(128)} %fusion.2.table, f32[2,512,512]{2,1,0:T(8,128)} %bitcast.17, f32[2,512,512]{2,1,0:T(8,128)} %copy-done.3, f32[2,512,512]{2,1,0:T(8,128)} %collective-permute-done.2.refs_2_, f32[2,512,512]{2,1,0:T(8,128)} %collective-permute-done.4.refs_3_, ...), custom_call_target="tpu_custom_call" | custom-call | flops 1024 | bytes 1024 | tf_op jit(solution)/shard_map/pallas_call | solution.py:118
  196.5 0.0 collective-permute-done.15.refs_9_.refs_13_.refs_6_.refs_10_
  196.5 0.0 copy-start.5
  196.5 0.0 collective-permute-done.16.refs_17_.refs_21_.refs_14_.refs_18_
  196.5 1.0 copy-done.5
  197.5 12.7 %shard_map.47 = (f32[2,512,512]{2,1,0:T(8,128)}, f32[2,512,512]{2,1,0:T(8,128)}) custom-call(s32[2]{0:T(128)} %fusion.1.table, f32[2,512,512]{2,1,0:T(8,128)} %bitcast.18, f32[2,512,512]{2,1,0:T(8,128)} %copy-done.3, f32[2,512,512]{2,1,0:T(8,128)} %collective-permute-done.2.refs_2_, f32[2,512,512]{2,1,0:T(8,128)} %collective-permute-done.4.refs_3_, ...), custom_call_target="tpu_custom_call" | custom-call | flops 1024 | bytes 1024 | tf_op jit(solution)/shard_map/pallas_call | solution.py:118
  210.2 0.0 collective-permute-done.7.refs_1_
  210.2 0.0 collective-permute-done.6.refs_0_
  210.2 0.0 collective-permute-done.12.refs_3_
  210.2 13.0 %shard_map.48 = (f32[2,512,512]{2,1,0:T(8,128)}, f32[2,512,512]{2,1,0:T(8,128)}) custom-call(s32[2]{0:T(128)} %fusion.table, f32[2,512,512]{2,1,0:T(8,128)} %collective-permute-done.6.refs_0_, f32[2,512,512]{2,1,0:T(8,128)} %collective-permute-done.7.refs_1_, f32[2,512,512]{2,1,0:T(8,128)} %collective-permute-done.11.refs_2_, ...), custom_call_target="tpu_custom_call" | custom-call | flops 1024 | bytes 1024 | tf_op jit(solution)/shard_map/pallas_call | solution.py:118
  223.2 3.8 %collective-permute-start.17 = (f32[2,512,512]{2,1,0:T(8,128)}, f32[2,512,512]{2,1,0:T(8,128)S(1)}, u32[]{:S(2)}, u32[]{:S(2)}) collective-permute-start(f32[2,512,512]{2,1,0:T(8,128)} %get-tuple-element.40), channel_id=1, source_target_pairs={{0,1},{1,0},{2,3},{3,2},{4,5},{5,4},{6,7},{7,6},{8,9},{9,8},{10,11... | collective-permute-start | bytes 6291464 | tf_op jit(solution)/shard_map/ppermute | solution.py:50
  227.0 4.0 %collective-permute-done.17 = f32[2,512,512]{2,1,0:T(8,128)S(1)} collective-permute-done((f32[2,512,512]{2,1,0:T(8,128)}, f32[2,512,512]{2,1,0:T(8,128)S(1)}, u32[]{:S(2)}, u32[]{:S(2)}) %collective-permute-start.17) | collective-permute-done | bytes 2097184 | tf_op jit(solution)/shard_map/ppermute | solution.py:50
  231.0 3.4 %add_bitcast_fusion = f32[1,2,512,512]{3,2,1,0:T(8,128)} fusion(f32[2,512,512]{2,1,0:T(8,128)} %get-tuple-element.39, f32[2,512,512]{2,1,0:T(8,128)S(1)} %collective-permute-done.17), kind=kLoop, calls=%fused_computation.1 | loop fusion | flops 524288 | bytes 6291456 | tf_op jit(solution)/shard_map/broadcast_in_dim | solution.py:205
Async XLA Ops:
  0.0 5.3 %copy-start.4 = (f32[1,2,512,512]{3,2,1,0:T(8,128)S(1)}, f32[1,2,512,512]{3,2,1,0:T(8,128)}, u32[]{:S(2)}) copy-start(f32[1,2,512,512]{3,2,1,0:T(8,128)} %param.4) | copy-start | bytes 6291460
  1.9 9.9 %collective-permute-start.8 = (f32[2,256,512]{2,1,0:T(8,128)S(1)}, f32[2,256,512]{2,1,0:T(8,128)S(1)}, u32[]{:S(2)}, u32[]{:S(2)}) collective-permute-start(f32[2,256,512]{2,1,0:T(8,128)S(1)} %get-tuple-element.41), channel_id=1, source_target_pairs={{0,1},{1,0},{2,3},{3,2},{4,5},{5,4},{6,7},{7,6},{8,9},{9,8},{10,11... | collective-permute-start | bytes 3145736 | tf_op jit(solution)/shard_map/ppermute | solution.py:50
  5.3 46.6 %collective-permute-start = (f32[2,512,512]{2,1,0:T(8,128)S(1)}, f32[2,512,512]{2,1,0:T(8,128)S(1)}, u32[]{:S(2)}, u32[]{:S(2)}) collective-permute-start(f32[2,512,512]{2,1,0:T(8,128)S(1)} %bitcast.19), channel_id=1, source_target_pairs={{0,2},{1,3},{2,4},{3,5},{4,6},{5,7},{6,32},{7,33},{64,66},{65,67},... | collective-permute-start | bytes 6291464 | tf_op jit(solution)/shard_map/ppermute | solution.py:42
  7.2 49.4 %collective-permute-start.1 = (f32[2,512,512]{2,1,0:T(8,128)S(1)}, f32[2,512,512]{2,1,0:T(8,128)}, u32[]{:S(2)}, u32[]{:S(2)}) collective-permute-start(f32[2,512,512]{2,1,0:T(8,128)S(1)} %bitcast.20), channel_id=1, source_target_pairs={{6,4},{7,5},{4,2},{5,3},{2,0},{3,1},{0,38},{1,39},{70,68},{71,69},... | collective-permute-start | bytes 6291464 | tf_op jit(solution)/shard_map/ppermute | solution.py:42
  11.8 1.6 copy-start.6
  13.4 52.8 %collective-permute-start.9 = (f32[2,2,256,512]{3,2,1,0:T(8,128)}, f32[2,2,256,512]{3,2,1,0:T(8,128)}, u32[]{:S(2)}, u32[]{:S(2)}) collective-permute-start(f32[2,2,256,512]{3,2,1,0:T(8,128)} %pad_maximum_fusion), channel_id=1, source_target_pairs={{32,0},{33,1},{38,6},{39,7},{96,64},{97,65},{102,70},{103,71},{160... | collective-permute-start | bytes 6291464 | tf_op jit(solution)/shard_map/ppermute | solution.py:42
  51.9 68.5 %copy-start.3 = (f32[2,512,512]{2,1,0:T(8,128)}, f32[2,512,512]{2,1,0:T(8,128)S(1)}, u32[]{:S(2)}) copy-start(f32[2,512,512]{2,1,0:T(8,128)S(1)} %collective-permute-done.refs_1_) | copy-start | bytes 6291460
  56.6 11.6 %collective-permute-start.2 = (f32[2,512,512]{2,1,0:T(8,128)S(1)}, f32[2,512,512]{2,1,0:T(8,128)}, u32[]{:S(2)}, u32[]{:S(2)}) collective-permute-start(f32[2,512,512]{2,1,0:T(8,128)S(1)} %collective-permute-done.refs_1_), channel_id=1, source_target_pairs={{4,6},{5,7},{6,32},{7,33},{32,34},{33,35},{68,70},{69,71},{70,96},... | collective-permute-start | bytes 6291464 | tf_op jit(solution)/shard_map/ppermute | solution.py:42
  58.7 49.6 %collective-permute-start.3 = (f32[2,512,512]{2,1,0:T(8,128)}, f32[2,512,512]{2,1,0:T(8,128)}, u32[]{:S(2)}, u32[]{:S(2)}) collective-permute-start(f32[2,512,512]{2,1,0:T(8,128)} %collective-permute-done.1.refs_4_), channel_id=1, source_target_pairs={{2,0},{3,1},{0,38},{1,39},{38,36},{39,37},{66,64},{67,65},{64,102}... | collective-permute-start | bytes 6291464 | tf_op jit(solution)/shard_map/ppermute | solution.py:42
  66.3 54.1 %collective-permute-start.10 = (f32[2,2,256,512]{3,2,1,0:T(8,128)}, f32[2,2,256,512]{3,2,1,0:T(8,128)}, u32[]{:S(2)}, u32[]{:S(2)}) collective-permute-start(f32[2,2,256,512]{3,2,1,0:T(8,128)} %pad_maximum_fusion), channel_id=1, source_target_pairs={{34,2},{35,3},{36,4},{37,5},{98,66},{99,67},{100,68},{101,69},{162... | collective-permute-start | bytes 6291464 | tf_op jit(solution)/shard_map/ppermute | solution.py:42
  108.3 48.6 %collective-permute-start.5 = (f32[2,512,512]{2,1,0:T(8,128)}, f32[2,512,512]{2,1,0:T(8,128)}, u32[]{:S(2)}, u32[]{:S(2)}) collective-permute-start(f32[2,512,512]{2,1,0:T(8,128)} %collective-permute-done.3.refs_5_), channel_id=1, source_target_pairs={{0,38},{1,39},{38,36},{39,37},{36,34},{37,35},{64,102},{65,103},{1... | collective-permute-start | bytes 6291464 | tf_op jit(solution)/shard_map/ppermute | solution.py:42
  115.0 41.9 %collective-permute-start.4 = (f32[2,512,512]{2,1,0:T(8,128)}, f32[2,512,512]{2,1,0:T(8,128)}, u32[]{:S(2)}, u32[]{:S(2)}) collective-permute-start(f32[2,512,512]{2,1,0:T(8,128)} %collective-permute-done.2.refs_2_), channel_id=1, source_target_pairs={{6,32},{7,33},{32,34},{33,35},{34,36},{35,37},{70,96},{71,97},{96,... | collective-permute-start | bytes 6291464 | tf_op jit(solution)/shard_map/ppermute | solution.py:42
  120.4 40.5 %collective-permute-start.11 = (f32[2,512,512]{2,1,0:T(8,128)}, f32[2,512,512]{2,1,0:T(8,128)}, u32[]{:S(2)}, u32[]{:S(2)}) collective-permute-start(f32[2,512,512]{2,1,0:T(8,128)} %broadcast_select_fusion), channel_id=1, source_target_pairs={{2,4},{3,5},{4,2},{5,3},{66,68},{67,69},{68,66},{69,67},{130,132},... | collective-permute-start | bytes 6291464 | tf_op jit(solution)/shard_map/ppermute | solution.py:42
  125.0 49.5 %copy-start = (f32[2,2,256,512]{3,2,1,0:T(8,128)}, f32[2,2,256,512]{3,2,1,0:T(8,128)S(1)}, u32[]{:S(2)}) copy-start(f32[2,2,256,512]{3,2,1,0:T(8,128)S(1)} %select_select_fusion.refs_7_.refs_10_.refs_13_.refs_16_.refs_11_.refs_15_.refs_19_.refs_4_.refs_8_.refs_12_) | copy-start | bytes 6291460
  125.0 46.2 %collective-permute-start.14 = (f32[2,2,256,512]{3,2,1,0:T(8,128)S(1)}, f32[2,2,256,512]{3,2,1,0:T(8,128)S(1)}, u32[]{:S(2)}, u32[]{:S(2)}) collective-permute-start(f32[2,2,256,512]{3,2,1,0:T(8,128)S(1)} %select_select_fusion.refs_7_.refs_10_.refs_13_.refs_16_.refs_11_.refs_15_.refs_19_.refs_4_.refs_8_.refs_12_), channel_id=1, source_target_pairs={{0,8},{8,16},{16,24},{24,0},{1,9},{9,17},{17,25},{25,1},{2,10},{10... | collective-permute-start | bytes 6291464 | tf_op jit(solution)/shard_map/ppermute | solution.py:152
  126.3 44.9 %collective-permute-start.13 = (f32[2,2,256,512]{3,2,1,0:T(8,128)S(1)}, f32[2,2,256,512]{3,2,1,0:T(8,128)S(1)}, u32[]{:S(2)}, u32[]{:S(2)}) collective-permute-start(f32[2,2,256,512]{3,2,1,0:T(8,128)S(1)} %select_select_fusion.refs_7_.refs_10_.refs_13_.refs_16_.refs_11_.refs_15_.refs_19_.refs_4_.refs_8_.refs_12_), channel_id=1, source_target_pairs={{0,24},{8,0},{16,8},{24,16},{1,25},{9,1},{17,9},{25,17},{2,26},{10... | collective-permute-start | bytes 6291464 | tf_op jit(solution)/shard_map/ppermute | solution.py:152
  156.9 53.3 %collective-permute-start.7 = (f32[2,512,512]{2,1,0:T(8,128)}, f32[2,512,512]{2,1,0:T(8,128)}, u32[]{:S(2)}, u32[]{:S(2)}) collective-permute-start(f32[2,512,512]{2,1,0:T(8,128)} %collective-permute-done.5.refs_6_), channel_id=1, source_target_pairs={{36,34},{37,35},{34,32},{35,33},{100,98},{101,99},{98,96},{99,97},... | collective-permute-start | bytes 6291464 | tf_op jit(solution)/shard_map/ppermute | solution.py:42
  158.9 51.3 %collective-permute-start.6 = (f32[2,512,512]{2,1,0:T(8,128)}, f32[2,512,512]{2,1,0:T(8,128)}, u32[]{:S(2)}, u32[]{:S(2)}) collective-permute-start(f32[2,512,512]{2,1,0:T(8,128)} %collective-permute-done.4.refs_3_), channel_id=1, source_target_pairs={{34,36},{35,37},{36,38},{37,39},{98,100},{99,101},{100,102},{101,1... | collective-permute-start | bytes 6291464 | tf_op jit(solution)/shard_map/ppermute | solution.py:42
  160.9 49.3 %collective-permute-start.12 = (f32[2,512,512]{2,1,0:T(8,128)}, f32[2,512,512]{2,1,0:T(8,128)}, u32[]{:S(2)}, u32[]{:S(2)}) collective-permute-start(f32[2,512,512]{2,1,0:T(8,128)} %collective-permute-done.11.refs_2_), channel_id=1, source_target_pairs={{4,6},{5,7},{2,0},{3,1},{68,70},{69,71},{66,64},{67,65},{132,134},... | collective-permute-start | bytes 6291464 | tf_op jit(solution)/shard_map/ppermute | solution.py:42
  171.2 3.3 %copy-start.1 = (f32[2,2,256,512]{3,2,1,0:T(8,128)}, f32[2,2,256,512]{3,2,1,0:T(8,128)S(1)}, u32[]{:S(2)}) copy-start(f32[2,2,256,512]{3,2,1,0:T(8,128)S(1)} %collective-permute-done.14.refs_9_.refs_12_.refs_15_.refs_18_.refs_10_.refs_14_.refs_22_.refs_7_.refs_11_.refs_19_) | copy-start | bytes 6291460
  171.2 2.2 copy-start.2
  172.4 24.1 %collective-permute-start.15 = (f32[2,256,512]{2,1,0:T(8,128)}, f32[2,256,512]{2,1,0:T(8,128)S(1)}, u32[]{:S(2)}, u32[]{:S(2)}) collective-permute-start(f32[2,256,512]{2,1,0:T(8,128)} %slice_bitcast_fusion.1), channel_id=1, source_target_pairs={{0,8},{8,16},{16,24},{24,0},{1,9},{9,17},{17,25},{25,1},{2,10},{10... | collective-permute-start | bytes 3145736 | tf_op jit(solution)/shard_map/ppermute | solution.py:152
  174.5 22.0 %collective-permute-start.16 = (f32[2,256,512]{2,1,0:T(8,128)}, f32[2,256,512]{2,1,0:T(8,128)}, u32[]{:S(2)}, u32[]{:S(2)}) collective-permute-start(f32[2,256,512]{2,1,0:T(8,128)} %slice_bitcast_fusion), channel_id=1, source_target_pairs={{0,24},{8,0},{16,8},{24,16},{1,25},{9,1},{17,9},{25,17},{2,26},{10... | collective-permute-start | bytes 3145736 | tf_op jit(solution)/shard_map/ppermute | solution.py:152
  196.5 1.0 copy-start.5
  223.2 7.8 %collective-permute-start.17 = (f32[2,512,512]{2,1,0:T(8,128)}, f32[2,512,512]{2,1,0:T(8,128)S(1)}, u32[]{:S(2)}, u32[]{:S(2)}) collective-permute-start(f32[2,512,512]{2,1,0:T(8,128)} %get-tuple-element.40), channel_id=1, source_target_pairs={{0,1},{1,0},{2,3},{3,2},{4,5},{5,4},{6,7},{7,6},{8,9},{9,8},{10,11... | collective-permute-start | bytes 6291464 | tf_op jit(solution)/shard_map/ppermute | solution.py:50

commit v5 on v4

--- a/solution.py
+++ b/solution.py
@@ -151,22 +151,25 @@
     def across(x, by):
         return lax.ppermute(x, "row", [(i, (i + by) % 4) for i in range(4)])
 
+    def halves(x):
+        low, high = x[:, :HALF], x[:, HALF:]
+        return jnp.stack([swap_cores(jnp.where(core == 0, high, low)), jnp.where(core == 0, low, high)])
+
     def both(x, pairs, *earlier):
         x = tuple(after(part, *earlier) if earlier else part for part in x)
         return ring_permute(x[0], pairs), ring_permute(x[1], mirrored(pairs))
 
     one = both((own, own), UP[0])
-    low, high = own[:, :HALF], own[:, HALF:]
-    kept = jnp.where(core == 0, low, high)
-    near = jnp.stack([swap_cores(jnp.where(core == 0, high, low)), kept])
-    crossed = ring_permute(near, CROSS[0])
+    crossed = ring_permute(own, CROSS[0])
+    source = halves(own)
     two = both(one, UP[1], *one)
-    crossed_late = ring_permute(after(near, *one, crossed), CROSS[1])
+    crossed_late = ring_permute(after(source, *one, crossed), CROSS[1])
     three = both(two, UP[2], *two)
     last = after(jnp.where(position == 1, *one), *two, crossed_late)
     last = ring_permute(last, LAST[0])
     inner = (position == 1) | (position == 2)
-    near = jnp.where(upper == 1, near, jnp.where(inner, after(crossed_late, *two), crossed))
+    crossed = halves(crossed)
+    near = jnp.where(upper == 1, source, jnp.where(inner, after(crossed_late, *two), crossed))
     right, left = across(near, 1), across(near, -1)
     four = both(three, UP[3], *three)
     very_last = ring_permute(after(last, *three), LAST[1])
@@ -201,8 +204,9 @@
     final = table_of(lambda early, late, r: late, late_bufs, (0, 1, 2, 3))
     total = products(early_ring, close, first)
     total = products(early_ring, second, third, total)
-    total = products(late_ring, second, final, total)
-    return (total[1] + swap_cores(total[0]))[None]
+    sent = swap_cores(total[0])
+    added = products(late_ring, second, final)
+    return (total[1] + sent + added[1] + swap_cores(added[0]))[None]
 
 
 def solution(mesh):

time: 235 us -> 229 us (0.974)
  waiting for transfers between devices: 126 us -> 114 us
  other arithmetic: 12.9 us -> 17.7 us
  starting transfers between devices: 46 us -> 50 us
  Pallas kernels: 42.2 us -> 39.8 us
    ppermute x12, waiting for transfers between devices: 113 us -> 104 us  [ring_permute(): return lax.ppermute(x, ('sec', 'col'), full)]
    ppermute x4, waiting for transfers between devices: 9.04 us -> 5.61 us  [across(): return lax.ppermute(x, 'row', [(i, (i + by) % 4) for i in range(4)])]
    select_n x2 -> x3, other arithmetic: 4.53 us -> 7.48 us  [the longest x2 4.86 us: halves(): jnp.where(core == 0, high, low)]
    pallas_call x3, Pallas kernels: 42.2 us -> 39.8 us  [products(): pl.pallas_call(functools.partial(product_kernel, slots, rows, len(bufs),...]
    ppermute x12, starting transfers between devices: 33.2 us -> 35.6 us  [ring_permute(): return lax.ppermute(x, ('sec', 'col'), full)]
    ppermute x2 -> x4, starting transfers between devices: 7.15 us -> 8.78 us  [swap_cores(): return lax.ppermute(x, 'col', [(i, i ^ 1) for i in range(8)])]
  transfers between devices with their start and end apart: 18 -> 20, of which waited for: 7 -> 6; matrix products, arithmetic and copies ran while one was open for 6% -> 8% of each run, Pallas kernels for 12% -> 17%
where the time goes in v5:
time: 229 us; the launch traced here: 228 us
  waiting for transfers between devices  114 us (50%)
  starting transfers between devices  50 us (22%)
  Pallas kernels  39.8 us (17%)
  other arithmetic  17.7 us (8%)
  local copies, waits for them, and re-layouts  6.92 us (3%)
    ppermute x12, waiting for transfers between devices, ring_permute(): return lax.ppermute(x, ('sec', 'col'), full)  104 us
    pallas_call x3, Pallas kernels, products(): pl.pallas_call(functools.partial(product_kernel, slots, rows, len(bufs),...  39.8 us
    ppermute x12, starting transfers between devices, ring_permute(): return lax.ppermute(x, ('sec', 'col'), full)  35.6 us
    ppermute x4, starting transfers between devices, swap_cores(): return lax.ppermute(x, 'col', [(i, i ^ 1) for i in range(8)])  8.78 us
    ppermute x4, waiting for transfers between devices, across(): return lax.ppermute(x, 'row', [(i, (i + by) % 4) for i in range(4)])  5.61 us
    ppermute x4, starting transfers between devices, across(): return lax.ppermute(x, 'row', [(i, (i + by) % 4) for i in range(4)])  5.6 us
    broadcast_in_dim x1, other arithmetic, shards(): return (total[1] + sent + added[1] + swap_cores(added[0]))[None]  5.21 us
    select_n x2, other arithmetic, halves(): jnp.where(core == 0, high, low)  4.86 us
  transfers between devices with their start and end apart: 20, of which 6 were waited for; matrix products, arithmetic and copies ran while one was open for 8% of the time, Pallas kernels for 17%

profile of v5, /device:TPU:1, one launch (start us, length us, event | category | flops | bytes accessed | tf_op | source)
XLA Modules:
  0.0 228.1 jit_solution(622895105471625461)
XLA Ops:
  0.0 4.5 %collective-permute-start = (f32[2,512,512]{2,1,0:T(8,128)}, f32[2,512,512]{2,1,0:T(8,128)S(1)}, u32[]{:S(2)}, u32[]{:S(2)}) collective-permute-start(f32[2,512,512]{2,1,0:T(8,128)} %bitcast.19), channel_id=1, source_target_pairs={{0,2},{1,3},{2,4},{3,5},{4,6},{5,7},{6,32},{7,33},{64,66},{65,67},... | collective-permute-start | bytes 6291464 | tf_op jit(solution)/shard_map/ppermute | solution.py:42
  4.5 4.6 %collective-permute-start.1 = (f32[2,512,512]{2,1,0:T(8,128)}, f32[2,512,512]{2,1,0:T(8,128)}, u32[]{:S(2)}, u32[]{:S(2)}) collective-permute-start(f32[2,512,512]{2,1,0:T(8,128)} %bitcast.20), channel_id=1, source_target_pairs={{6,4},{7,5},{4,2},{5,3},{2,0},{3,1},{0,38},{1,39},{70,68},{71,69},... | collective-permute-start | bytes 6291464 | tf_op jit(solution)/shard_map/ppermute | solution.py:42
  9.1 1.3 collective-permute-start.7
  10.4 1.8 slice_select_fusion.1
  12.2 1.0 collective-permute-start.6
  13.3 35.7 %collective-permute-done.refs_1_ = f32[2,512,512]{2,1,0:T(8,128)S(1)} collective-permute-done((f32[2,512,512]{2,1,0:T(8,128)}, f32[2,512,512]{2,1,0:T(8,128)S(1)}, u32[]{:S(2)}, u32[]{:S(2)}) %collective-permute-start) | collective-permute-done | bytes 2097184 | tf_op jit(solution)/shard_map/ppermute | solution.py:42
  49.0 0.0 copy-start.3
  49.0 4.7 %collective-permute-done.1.refs_4_ = f32[2,512,512]{2,1,0:T(8,128)} collective-permute-done((f32[2,512,512]{2,1,0:T(8,128)}, f32[2,512,512]{2,1,0:T(8,128)}, u32[]{:S(2)}, u32[]{:S(2)}) %collective-permute-start.1) | collective-permute-done | bytes 2097184 | tf_op jit(solution)/shard_map/ppermute | solution.py:42
  53.7 2.0 collective-permute-start.2
  55.7 5.3 %collective-permute-start.3 = (f32[2,512,512]{2,1,0:T(8,128)}, f32[2,512,512]{2,1,0:T(8,128)}, u32[]{:S(2)}, u32[]{:S(2)}) collective-permute-start(f32[2,512,512]{2,1,0:T(8,128)} %collective-permute-done.1.refs_4_), channel_id=1, source_target_pairs={{2,0},{3,1},{0,38},{1,39},{38,36},{39,37},{66,64},{67,65},{64,102}... | collective-permute-start | bytes 6291464 | tf_op jit(solution)/shard_map/ppermute | solution.py:42
  61.0 0.0 collective-permute-done.6
  61.0 0.0 copy-start.5
  61.0 1.7 pad_maximum_fusion
  62.7 0.0 copy-done.5
  62.7 0.0 collective-permute-done.7
  62.7 2.0 collective-permute-start.8
  64.6 3.1 %slice_select_fusion = (f32[2,256,512]{2,1,0:T(8,128)}, f32[1,2,256,512]{3,2,1,0:T(8,128)}) fusion(f32[2,512,512]{2,1,0:T(8,128)} %collective-permute-done.7, pred[]{:T(512)S(6)} %eq.20), kind=kLoop, calls=%fused_computation.9 | loop fusion | flops 524288 | bytes 4194305 | tf_op jit(solution)/shard_map/jit(_where)/select_n | solution.py:156
  67.7 2.1 collective-permute-start.9
  69.8 0.0 copy-done.3
  69.8 3.4 %broadcast_select_fusion = f32[2,512,512]{2,1,0:T(8,128)} fusion(f32[2,512,512]{2,1,0:T(8,128)S(1)} %collective-permute-done.refs_1_, f32[2,512,512]{2,1,0:T(8,128)} %collective-permute-done.1.refs_4_, pred[]{:T(512)S(6)} %eq.21), kind=kLoop, calls=%fused_computation.8 | loop fusion | flops 524288 | bytes 6291457 | tf_op jit(solution)/shard_map/jit(_where)/select_n | solution.py:168
  73.2 0.0 collective-permute-done.2.refs_2_
  73.2 31.4 %collective-permute-done.3.refs_5_ = f32[2,512,512]{2,1,0:T(8,128)} collective-permute-done((f32[2,512,512]{2,1,0:T(8,128)}, f32[2,512,512]{2,1,0:T(8,128)}, u32[]{:S(2)}, u32[]{:S(2)}) %collective-permute-start.3) | collective-permute-done | bytes 2097184 | tf_op jit(solution)/shard_map/ppermute | solution.py:42
  104.7 6.6 %collective-permute-start.5 = (f32[2,512,512]{2,1,0:T(8,128)}, f32[2,512,512]{2,1,0:T(8,128)}, u32[]{:S(2)}, u32[]{:S(2)}) collective-permute-start(f32[2,512,512]{2,1,0:T(8,128)} %collective-permute-done.3.refs_5_), channel_id=1, source_target_pairs={{0,38},{1,39},{38,36},{39,37},{36,34},{37,35},{64,102},{65,103},{1... | collective-permute-start | bytes 6291464 | tf_op jit(solution)/shard_map/ppermute | solution.py:42
  111.3 2.0 collective-permute-start.4
  113.3 0.0 collective-permute-done.8
  113.3 2.0 collective-permute-start.17
  115.3 0.0 collective-permute-done.9
  115.3 2.6 %fusion.refs_7_.refs_10_.refs_13_.refs_16_.refs_11_.refs_15_.refs_19_.refs_4_.refs_8_.refs_12_ = f32[2,2,256,512]{3,2,1,0:T(8,128)S(1)} fusion(f32[2,2,256,512]{3,2,1,0:T(8,128)} %collective-permute-done.8, f32[1,2,256,512]{3,2,1,0:T(8,128)} %get-tuple-element.42, f32[1,2,256,512]{3,2,1,0:T(8,128)} %bitcast.4, pred[]{:T(512)S(6)} %or.3, pred[]{:T(512)S(6)} %eq.19, ...), kind=kLoop, calls=%fused_computation.2 | loop fusion | flops 2097152 | bytes 8388610 | tf_op jit(solution)/shard_map/jit(_where)/select_n | solution.py:172
  117.9 0.0 copy-start
  118.0 1.3 collective-permute-start.11
  119.2 1.5 collective-permute-start.10
  120.7 32.0 %collective-permute-done.5.refs_6_ = f32[2,512,512]{2,1,0:T(8,128)} collective-permute-done((f32[2,512,512]{2,1,0:T(8,128)}, f32[2,512,512]{2,1,0:T(8,128)}, u32[]{:S(2)}, u32[]{:S(2)}) %collective-permute-start.5) | collective-permute-done | bytes 2097184 | tf_op jit(solution)/shard_map/ppermute | solution.py:42
  152.7 0.0 collective-permute-done.4.refs_3_
  152.7 0.0 collective-permute-done.17.refs_2_
  152.7 1.3 collective-permute-start.18
  154.0 2.0 collective-permute-start.16
  156.0 2.0 collective-permute-start.15
  158.0 5.6 %collective-permute-done.11.refs_9_.refs_12_.refs_15_.refs_18_.refs_10_.refs_14_.refs_22_.refs_7_.refs_11_.refs_19_ = f32[2,2,256,512]{3,2,1,0:T(8,128)S(1)} collective-permute-done((f32[2,2,256,512]{3,2,1,0:T(8,128)S(1)}, f32[2,2,256,512]{3,2,1,0:T(8,128)S(1)}, u32[]{:S(2)}, u32[]{:S(2)}) %collective-permute-start.11) | collective-permute-done | bytes 2097184 | tf_op jit(solution)/shard_map/ppermute | solution.py:152
  163.6 0.0 collective-permute-done.10.refs_8_.refs_11_.refs_14_.refs_17_.refs_12_.refs_16_.refs_20_.refs_5_.refs_9_.refs_13_
  163.6 1.2 slice_bitcast_fusion.1
  164.8 0.9 collective-permute-start.12
  165.7 0.0 copy-done.2
  165.7 1.1 slice_bitcast_fusion
  166.8 0.0 copy-done
  166.8 0.0 copy-done.1
  166.8 1.9 collective-permute-start.13
  168.8 1.2 fusion.2.table
  169.9 1.2 fusion.1.table
  171.2 1.2 fusion.3.table
  172.4 16.5 %shard_map.46 = (f32[2,512,512]{2,1,0:T(8,128)}, f32[2,512,512]{2,1,0:T(8,128)}) custom-call(s32[4]{0:T(128)} %fusion.2.table, f32[2,512,512]{2,1,0:T(8,128)} %bitcast.23, f32[2,512,512]{2,1,0:T(8,128)} %copy-done.3, f32[2,512,512]{2,1,0:T(8,128)} %collective-permute-done.2.refs_2_, f32[2,512,512]{2,1,0:T(8,128)} %collective-permute-done.4.refs_3_, ...), custom_call_target="tpu_custom_call" | custom-call | flops 1024 | bytes 1024 | tf_op jit(solution)/shard_map/pallas_call | solution.py:118
  188.9 0.0 collective-permute-done.12.refs_9_.refs_13_.refs_6_.refs_10_
  188.9 0.0 copy-start.4
  188.9 0.0 collective-permute-done.13.refs_17_.refs_21_.refs_14_.refs_18_
  188.9 1.0 copy-done.4
  189.9 12.7 %shard_map.47 = (f32[2,512,512]{2,1,0:T(8,128)}, f32[2,512,512]{2,1,0:T(8,128)}) custom-call(s32[2]{0:T(128)} %fusion.1.table, f32[2,512,512]{2,1,0:T(8,128)} %bitcast.24, f32[2,512,512]{2,1,0:T(8,128)} %copy-done.3, f32[2,512,512]{2,1,0:T(8,128)} %collective-permute-done.2.refs_2_, f32[2,512,512]{2,1,0:T(8,128)} %collective-permute-done.4.refs_3_, ...), custom_call_target="tpu_custom_call" | custom-call | flops 1024 | bytes 1024 | tf_op jit(solution)/shard_map/pallas_call | solution.py:118
  202.6 4.6 %collective-permute-start.14 = (f32[2,512,512]{2,1,0:T(8,128)}, f32[2,512,512]{2,1,0:T(8,128)}, u32[]{:S(2)}, u32[]{:S(2)}) collective-permute-start(f32[2,512,512]{2,1,0:T(8,128)} %get-tuple-element.34), channel_id=1, source_target_pairs={{0,1},{1,0},{2,3},{3,2},{4,5},{5,4},{6,7},{7,6},{8,9},{9,8},{10,11... | collective-permute-start | bytes 6291464 | tf_op jit(solution)/shard_map/ppermute | solution.py:50
  207.2 0.0 collective-permute-done.18.refs_3_
  207.2 0.0 collective-permute-done.16.refs_1_
  207.2 0.0 collective-permute-done.15.refs_0_
  207.2 10.6 %shard_map.48 = (f32[2,512,512]{2,1,0:T(8,128)}, f32[2,512,512]{2,1,0:T(8,128)}) custom-call(s32[2]{0:T(128)} %fusion.3.table, f32[2,512,512]{2,1,0:T(8,128)} %collective-permute-done.15.refs_0_, f32[2,512,512]{2,1,0:T(8,128)} %collective-permute-done.16.refs_1_, f32[2,512,512]{2,1,0:T(8,128)} %collective-permute-done.17.refs_2_, ...), custom_call_target="tpu_custom_call" | custom-call | flops 1024 | bytes 1024 | tf_op jit(solution)/shard_map/pallas_call | solution.py:118
  217.8 1.1 collective-permute-start.19
  218.9 0.0 collective-permute-done.14
  218.9 4.0 %collective-permute-done.19 = f32[2,512,512]{2,1,0:T(8,128)S(1)} collective-permute-done((f32[2,512,512]{2,1,0:T(8,128)}, f32[2,512,512]{2,1,0:T(8,128)S(1)}, u32[]{:S(2)}, u32[]{:S(2)}) %collective-permute-start.19) | collective-permute-done | bytes 2097184 | tf_op jit(solution)/shard_map/ppermute | solution.py:50
  222.9 5.2 %add_bitcast_fusion = f32[1,2,512,512]{3,2,1,0:T(8,128)} fusion(f32[2,512,512]{2,1,0:T(8,128)S(1)} %collective-permute-done.19, f32[2,512,512]{2,1,0:T(8,128)} %get-tuple-element.39, f32[2,512,512]{2,1,0:T(8,128)} %get-tuple-element.33, f32[2,512,512]{2,1,0:T(8,128)} %collective-permute-done.14), kind=kLoop, calls=%fused_computation.3 | loop fusion | flops 1572864 | bytes 10485760 | tf_op jit(solution)/shard_map/broadcast_in_dim | solution.py:209
  (2 shorter events, 0.0 us)
Async XLA Ops:
  0.0 49.0 %collective-permute-start = (f32[2,512,512]{2,1,0:T(8,128)}, f32[2,512,512]{2,1,0:T(8,128)S(1)}, u32[]{:S(2)}, u32[]{:S(2)}) collective-permute-start(f32[2,512,512]{2,1,0:T(8,128)} %bitcast.19), channel_id=1, source_target_pairs={{0,2},{1,3},{2,4},{3,5},{4,6},{5,7},{6,32},{7,33},{64,66},{65,67},... | collective-permute-start | bytes 6291464 | tf_op jit(solution)/shard_map/ppermute | solution.py:42
  4.5 49.2 %collective-permute-start.1 = (f32[2,512,512]{2,1,0:T(8,128)}, f32[2,512,512]{2,1,0:T(8,128)}, u32[]{:S(2)}, u32[]{:S(2)}) collective-permute-start(f32[2,512,512]{2,1,0:T(8,128)} %bitcast.20), channel_id=1, source_target_pairs={{6,4},{7,5},{4,2},{5,3},{2,0},{3,1},{0,38},{1,39},{70,68},{71,69},... | collective-permute-start | bytes 6291464 | tf_op jit(solution)/shard_map/ppermute | solution.py:42
  9.1 53.5 %collective-permute-start.7 = (f32[2,512,512]{2,1,0:T(8,128)}, f32[2,512,512]{2,1,0:T(8,128)}, u32[]{:S(2)}, u32[]{:S(2)}) collective-permute-start(f32[2,512,512]{2,1,0:T(8,128)} %bitcast.21), channel_id=1, source_target_pairs={{32,0},{33,1},{38,6},{39,7},{96,64},{97,65},{102,70},{103,71},{160... | collective-permute-start | bytes 6291464 | tf_op jit(solution)/shard_map/ppermute | solution.py:42
  12.2 48.8 %collective-permute-start.6 = (f32[2,256,512]{2,1,0:T(8,128)S(1)}, f32[2,256,512]{2,1,0:T(8,128)S(1)}, u32[]{:S(2)}, u32[]{:S(2)}) collective-permute-start(f32[2,256,512]{2,1,0:T(8,128)S(1)} %get-tuple-element.43), channel_id=1, source_target_pairs={{0,1},{1,0},{2,3},{3,2},{4,5},{5,4},{6,7},{7,6},{8,9},{9,8},{10,11... | collective-permute-start | bytes 3145736 | tf_op jit(solution)/shard_map/ppermute | solution.py:50
  49.0 20.9 %copy-start.3 = (f32[2,512,512]{2,1,0:T(8,128)}, f32[2,512,512]{2,1,0:T(8,128)S(1)}, u32[]{:S(2)}) copy-start(f32[2,512,512]{2,1,0:T(8,128)S(1)} %collective-permute-done.refs_1_) | copy-start | bytes 6291460
  53.7 19.5 %collective-permute-start.2 = (f32[2,512,512]{2,1,0:T(8,128)S(1)}, f32[2,512,512]{2,1,0:T(8,128)}, u32[]{:S(2)}, u32[]{:S(2)}) collective-permute-start(f32[2,512,512]{2,1,0:T(8,128)S(1)} %collective-permute-done.refs_1_), channel_id=1, source_target_pairs={{4,6},{5,7},{6,32},{7,33},{32,34},{33,35},{68,70},{69,71},{70,96},... | collective-permute-start | bytes 6291464 | tf_op jit(solution)/shard_map/ppermute | solution.py:42
  55.7 49.0 %collective-permute-start.3 = (f32[2,512,512]{2,1,0:T(8,128)}, f32[2,512,512]{2,1,0:T(8,128)}, u32[]{:S(2)}, u32[]{:S(2)}) collective-permute-start(f32[2,512,512]{2,1,0:T(8,128)} %collective-permute-done.1.refs_4_), channel_id=1, source_target_pairs={{2,0},{3,1},{0,38},{1,39},{38,36},{39,37},{66,64},{67,65},{64,102}... | collective-permute-start | bytes 6291464 | tf_op jit(solution)/shard_map/ppermute | solution.py:42
  61.0 1.7 copy-start.5
  62.7 50.6 %collective-permute-start.8 = (f32[2,2,256,512]{3,2,1,0:T(8,128)}, f32[2,2,256,512]{3,2,1,0:T(8,128)}, u32[]{:S(2)}, u32[]{:S(2)}) collective-permute-start(f32[2,2,256,512]{3,2,1,0:T(8,128)} %pad_maximum_fusion), channel_id=1, source_target_pairs={{34,2},{35,3},{36,4},{37,5},{98,66},{99,67},{100,68},{101,69},{162... | collective-permute-start | bytes 6291464 | tf_op jit(solution)/shard_map/ppermute | solution.py:42
  67.7 47.6 %collective-permute-start.9 = (f32[2,256,512]{2,1,0:T(8,128)}, f32[2,256,512]{2,1,0:T(8,128)}, u32[]{:S(2)}, u32[]{:S(2)}) collective-permute-start(f32[2,256,512]{2,1,0:T(8,128)} %get-tuple-element.41), channel_id=1, source_target_pairs={{0,1},{1,0},{2,3},{3,2},{4,5},{5,4},{6,7},{7,6},{8,9},{9,8},{10,11... | collective-permute-start | bytes 3145736 | tf_op jit(solution)/shard_map/ppermute | solution.py:50
  104.7 48.1 %collective-permute-start.5 = (f32[2,512,512]{2,1,0:T(8,128)}, f32[2,512,512]{2,1,0:T(8,128)}, u32[]{:S(2)}, u32[]{:S(2)}) collective-permute-start(f32[2,512,512]{2,1,0:T(8,128)} %collective-permute-done.3.refs_5_), channel_id=1, source_target_pairs={{0,38},{1,39},{38,36},{39,37},{36,34},{37,35},{64,102},{65,103},{1... | collective-permute-start | bytes 6291464 | tf_op jit(solution)/shard_map/ppermute | solution.py:42
  111.3 41.4 %collective-permute-start.4 = (f32[2,512,512]{2,1,0:T(8,128)}, f32[2,512,512]{2,1,0:T(8,128)}, u32[]{:S(2)}, u32[]{:S(2)}) collective-permute-start(f32[2,512,512]{2,1,0:T(8,128)} %collective-permute-done.2.refs_2_), channel_id=1, source_target_pairs={{6,32},{7,33},{32,34},{33,35},{34,36},{35,37},{70,96},{71,97},{96,... | collective-permute-start | bytes 6291464 | tf_op jit(solution)/shard_map/ppermute | solution.py:42
  113.3 39.4 %collective-permute-start.17 = (f32[2,512,512]{2,1,0:T(8,128)}, f32[2,512,512]{2,1,0:T(8,128)}, u32[]{:S(2)}, u32[]{:S(2)}) collective-permute-start(f32[2,512,512]{2,1,0:T(8,128)} %broadcast_select_fusion), channel_id=1, source_target_pairs={{2,4},{3,5},{4,2},{5,3},{66,68},{67,69},{68,66},{69,67},{130,132},... | collective-permute-start | bytes 6291464 | tf_op jit(solution)/shard_map/ppermute | solution.py:42
  117.9 48.9 %copy-start = (f32[2,2,256,512]{3,2,1,0:T(8,128)}, f32[2,2,256,512]{3,2,1,0:T(8,128)S(1)}, u32[]{:S(2)}) copy-start(f32[2,2,256,512]{3,2,1,0:T(8,128)S(1)} %fusion.refs_7_.refs_10_.refs_13_.refs_16_.refs_11_.refs_15_.refs_19_.refs_4_.refs_8_.refs_12_) | copy-start | bytes 6291460
  118.0 45.7 %collective-permute-start.11 = (f32[2,2,256,512]{3,2,1,0:T(8,128)S(1)}, f32[2,2,256,512]{3,2,1,0:T(8,128)S(1)}, u32[]{:S(2)}, u32[]{:S(2)}) collective-permute-start(f32[2,2,256,512]{3,2,1,0:T(8,128)S(1)} %fusion.refs_7_.refs_10_.refs_13_.refs_16_.refs_11_.refs_15_.refs_19_.refs_4_.refs_8_.refs_12_), channel_id=1, source_target_pairs={{0,8},{8,16},{16,24},{24,0},{1,9},{9,17},{17,25},{25,1},{2,10},{10... | collective-permute-start | bytes 6291464 | tf_op jit(solution)/shard_map/ppermute | solution.py:152
  119.2 44.4 %collective-permute-start.10 = (f32[2,2,256,512]{3,2,1,0:T(8,128)S(1)}, f32[2,2,256,512]{3,2,1,0:T(8,128)S(1)}, u32[]{:S(2)}, u32[]{:S(2)}) collective-permute-start(f32[2,2,256,512]{3,2,1,0:T(8,128)S(1)} %fusion.refs_7_.refs_10_.refs_13_.refs_16_.refs_11_.refs_15_.refs_19_.refs_4_.refs_8_.refs_12_), channel_id=1, source_target_pairs={{0,24},{8,0},{16,8},{24,16},{1,25},{9,1},{17,9},{25,17},{2,26},{10... | collective-permute-start | bytes 6291464 | tf_op jit(solution)/shard_map/ppermute | solution.py:152
  152.7 54.5 %collective-permute-start.18 = (f32[2,512,512]{2,1,0:T(8,128)}, f32[2,512,512]{2,1,0:T(8,128)}, u32[]{:S(2)}, u32[]{:S(2)}) collective-permute-start(f32[2,512,512]{2,1,0:T(8,128)} %collective-permute-done.17.refs_2_), channel_id=1, source_target_pairs={{4,6},{5,7},{2,0},{3,1},{68,70},{69,71},{66,64},{67,65},{132,134},... | collective-permute-start | bytes 6291464 | tf_op jit(solution)/shard_map/ppermute | solution.py:42
  154.0 53.2 %collective-permute-start.16 = (f32[2,512,512]{2,1,0:T(8,128)}, f32[2,512,512]{2,1,0:T(8,128)}, u32[]{:S(2)}, u32[]{:S(2)}) collective-permute-start(f32[2,512,512]{2,1,0:T(8,128)} %collective-permute-done.5.refs_6_), channel_id=1, source_target_pairs={{36,34},{37,35},{34,32},{35,33},{100,98},{101,99},{98,96},{99,97},... | collective-permute-start | bytes 6291464 | tf_op jit(solution)/shard_map/ppermute | solution.py:42
  156.0 51.2 %collective-permute-start.15 = (f32[2,512,512]{2,1,0:T(8,128)}, f32[2,512,512]{2,1,0:T(8,128)}, u32[]{:S(2)}, u32[]{:S(2)}) collective-permute-start(f32[2,512,512]{2,1,0:T(8,128)} %collective-permute-done.4.refs_3_), channel_id=1, source_target_pairs={{34,36},{35,37},{36,38},{37,39},{98,100},{99,101},{100,102},{101,1... | collective-permute-start | bytes 6291464 | tf_op jit(solution)/shard_map/ppermute | solution.py:42
  163.6 3.2 %copy-start.1 = (f32[2,2,256,512]{3,2,1,0:T(8,128)}, f32[2,2,256,512]{3,2,1,0:T(8,128)S(1)}, u32[]{:S(2)}) copy-start(f32[2,2,256,512]{3,2,1,0:T(8,128)S(1)} %collective-permute-done.11.refs_9_.refs_12_.refs_15_.refs_18_.refs_10_.refs_14_.refs_22_.refs_7_.refs_11_.refs_19_) | copy-start | bytes 6291460
  163.6 2.1 copy-start.2
  164.8 24.1 %collective-permute-start.12 = (f32[2,256,512]{2,1,0:T(8,128)}, f32[2,256,512]{2,1,0:T(8,128)S(1)}, u32[]{:S(2)}, u32[]{:S(2)}) collective-permute-start(f32[2,256,512]{2,1,0:T(8,128)} %slice_bitcast_fusion.1), channel_id=1, source_target_pairs={{0,8},{8,16},{16,24},{24,0},{1,9},{9,17},{17,25},{25,1},{2,10},{10... | collective-permute-start | bytes 3145736 | tf_op jit(solution)/shard_map/ppermute | solution.py:152
  166.8 22.1 %collective-permute-start.13 = (f32[2,256,512]{2,1,0:T(8,128)}, f32[2,256,512]{2,1,0:T(8,128)}, u32[]{:S(2)}, u32[]{:S(2)}) collective-permute-start(f32[2,256,512]{2,1,0:T(8,128)} %slice_bitcast_fusion), channel_id=1, source_target_pairs={{0,24},{8,0},{16,8},{24,16},{1,25},{9,1},{17,9},{25,17},{2,26},{10... | collective-permute-start | bytes 3145736 | tf_op jit(solution)/shard_map/ppermute | solution.py:152
  188.9 1.0 copy-start.4
  202.6 16.2 %collective-permute-start.14 = (f32[2,512,512]{2,1,0:T(8,128)}, f32[2,512,512]{2,1,0:T(8,128)}, u32[]{:S(2)}, u32[]{:S(2)}) collective-permute-start(f32[2,512,512]{2,1,0:T(8,128)} %get-tuple-element.34), channel_id=1, source_target_pairs={{0,1},{1,0},{2,3},{3,2},{4,5},{5,4},{6,7},{7,6},{8,9},{9,8},{10,11... | collective-permute-start | bytes 6291464 | tf_op jit(solution)/shard_map/ppermute | solution.py:50
  217.8 5.1 %collective-permute-start.19 = (f32[2,512,512]{2,1,0:T(8,128)}, f32[2,512,512]{2,1,0:T(8,128)S(1)}, u32[]{:S(2)}, u32[]{:S(2)}) collective-permute-start(f32[2,512,512]{2,1,0:T(8,128)} %get-tuple-element.40), channel_id=1, source_target_pairs={{0,1},{1,0},{2,3},{3,2},{4,5},{5,4},{6,7},{7,6},{8,9},{9,8},{10,11... | collective-permute-start | bytes 6291464 | tf_op jit(solution)/shard_map/ppermute | solution.py:50
